TPU v7x, 256 devices: a whole 4x4x8 slice. The times are simulated.
256 devices in a mesh: samp: 32 (over z, x), feat: 8 (over y, core).
Axes of the slice: x: 4, y: 4, z: 8, core: 2. Of those that a mesh axis runs over, the one named last changes fastest.
Arguments:
- features: float32 [32768, 16384], P('samp', 'feat'), as said below
- targets: float32 [32768, 64], P('samp'), may hold values from -6 to 6
- ridge: float32 [64], replicated, may hold values from 0.5 to 5
Outputs:
- solution: float32 [16384, 64], P('feat')
- residual: float32 [32768, 64], P('samp')
Inputs may be any that keep to these rules, and one draw needn't show every extreme that they name: `features`: rows and columns carry independent positive scales; entries are finite.
All inputs are finite; a program needn't handle non-finite values.
Results may differ from a plain program's by a relative error of at most 0.0004.
Values sent between devices are 32-bit elements; how exact they have to be, the bound alone decides.
No kernel may reach another device: no remote copies, remote signals or barrier semaphores. Data moves between devices by JAX's collectives and lax.ppermute only.
A program may use at most 64 MiB of HBM per device.

v0:
```python
import jax
import jax.numpy as jnp
from jax import lax
from jax.sharding import PartitionSpec as P

ITERS = 3


def colsq(values):
    return jnp.sum(values * values, axis=0)


def per_device(features, targets, ridge):
    high = lax.Precision.HIGHEST
    first_samp = lax.axis_index("samp") == 0
    first_feat = lax.axis_index("feat") == 0
    width = targets.shape[1]

    def transposed(residual_full):
        return lax.dot_general(
            features,
            residual_full,
            (((0,), (0,)), ((), ())),
            precision=high,
            preferred_element_type=jnp.float32,
        )

    def gradient_of(residual_full):
        return lax.psum(transposed(residual_full), "samp")

    def gradient_sq(gradient):
        local = colsq(gradient)
        local = jnp.where(first_samp, local, jnp.zeros_like(local))
        return lax.psum(local, ("samp", "feat"))

    residual = targets
    gradient = gradient_of(targets)
    solution = jnp.zeros_like(gradient)
    direction = gradient
    gamma = gradient_sq(gradient)
    for step in range(ITERS):
        full_dir = direction
        partial_value = jnp.dot(
            features, full_dir, precision=high, preferred_element_type=jnp.float32
        )
        image = lax.psum(partial_value, "feat")
        image_sq = jnp.where(first_feat, colsq(image), jnp.zeros((width,), jnp.float32))
        dir_sq = colsq(direction)
        dir_sq = jnp.where(first_samp, dir_sq, jnp.zeros_like(dir_sq))
        total_image, total_dir = lax.psum((image_sq, dir_sq), ("samp", "feat"))
        alpha = gamma / (total_image + ridge * total_dir)
        solution = solution + alpha * direction
        residual = residual - alpha * image
        if step + 1 < ITERS:
            gradient = gradient_of(residual) - ridge * solution
            fresh = gradient_sq(gradient)
            direction = gradient + fresh / gamma * direction
            gamma = fresh
    return (solution, residual)


def solution(mesh):
    placed = (P("samp", "feat"), P("samp", None), P())
    return jax.shard_map(
        per_device,
        mesh=mesh,
        in_specs=placed,
        out_specs=(P("feat", None), P("samp", None)),
        check_vma=False,
    )
```

profile of v0, /device:TPU:1, one launch (start us, length us, event | category | flops | bytes accessed | tf_op | source)
XLA Modules:
  0.0 1088.5 jit_solution(221311810953601343)
XLA Ops:
  7.2 9.6 fusion
  16.8 0.0 all-reduce.12.cloned.1.call-start
  16.9 146.7 %all-reduce.10.cloned.1.call-done = f32[2048,64]{0,1:T(8,128)} async-done(((f32[2048,64]{0,1:T(8,128)}), f32[2048,64]{0,1:T(8,128)}) %all-reduce.10.cloned.1.call-update) | async-done | bytes 524304 | tf_op jit(solution)/shard_map/psum | solution.py:29
  163.6 12.3 %convolution_bitcast_fusion.4 = f32[1024,64]{0,1:T(8,128)} fusion(f32[2048,64]{0,1:T(8,128)} %all-reduce.10.cloned.1.call-done, f32[1024,2048]{1,0:T(8,128)} %param.3), kind=kOutput, calls=%fused_computation.4 | convolution fusion | flops 1610612736 | bytes 9175040 | tf_op jit(solution)/shard_map/dot_general | solution.py:43
  175.9 0.0 all-reduce.14.cloned.1.call-start
  176.0 0.1 multiply_reduce_fusion.4
  176.1 64.4 %all-reduce.12.cloned.1.call-done = f32[1024,64]{0,1:T(8,128)} async-done(((f32[1024,64]{0,1:T(8,128)}), f32[1024,64]{0,1:T(8,128)}) %all-reduce.12.cloned.1.call-update) | async-done | bytes 262160 | tf_op jit(solution)/shard_map/psum | solution.py:46
  240.5 1.1 multiply_reduce_fusion.7
  241.6 78.5 %all-reduce.2 = (f32[64]{0:T(128)S(1)}, f32[64]{0:T(128)S(1)}) all-reduce(f32[64]{0:T(128)S(1)} %broadcast_select_fusion.7, f32[64]{0:T(128)S(1)} %broadcast_select_fusion.2), channel_id=1, replica_groups=mesh['samp'=32,'feat'=8] {'samp','feat'}, use_global_device_ids=true, to_apply=%region_2.3 | all-reduce | flops 128 | bytes 1024 | tf_op jit(solution)/shard_map/psum | solution.py:34
  320.2 9.4 convolution_bitcast_fusion.1
  329.7 139.3 %all-reduce.14.cloned.1.call-done = f32[2048,64]{0,1:T(8,128)} async-done(((f32[2048,64]{0,1:T(8,128)}), f32[2048,64]{0,1:T(8,128)}) %all-reduce.14.cloned.1.call-update) | async-done | bytes 524304 | tf_op jit(solution)/shard_map/psum | solution.py:29
  468.9 1.3 multiply_reduce_fusion.3
  470.3 78.9 %psum.106 = f32[64]{0:T(128)S(1)} all-reduce(f32[64]{0:T(128)S(1)} %broadcast_select_fusion.6), channel_id=1, replica_groups=mesh['samp'=32,'feat'=8] {'samp','feat'}, use_global_device_ids=true, to_apply=%region_8.9 | all-reduce | flops 64 | bytes 512 | tf_op jit(solution)/shard_map/psum | solution.py:34
  549.2 1.4 multiply_reduce_fusion.2
  550.5 11.1 %convolution_bitcast_fusion.3 = f32[1024,64]{0,1:T(8,128)} fusion(f32[2048,64]{0,1:T(8,128)S(1)} %get-tuple-element.11, f32[1024,2048]{1,0:T(8,128)} %param.3), kind=kOutput, calls=%fused_computation.3 | convolution fusion | flops 1610612736 | bytes 9175040 | tf_op jit(solution)/shard_map/dot_general | solution.py:43
  561.6 0.0 all-reduce.18.cloned.1.call-start
  561.7 58.3 %all-reduce.16.cloned.1.call-done = f32[1024,64]{0,1:T(8,128)} async-done(((f32[1024,64]{0,1:T(8,128)}), f32[1024,64]{0,1:T(8,128)}) %all-reduce.16.cloned.1.call-update) | async-done | bytes 262160 | tf_op jit(solution)/shard_map/psum | solution.py:46
  620.0 1.1 multiply_reduce_fusion.6
  621.1 78.6 %all-reduce.1 = (f32[64]{0:T(128)S(1)}, f32[64]{0:T(128)S(1)}) all-reduce(f32[64]{0:T(128)S(1)} %broadcast_select_fusion.1, f32[64]{0:T(128)S(1)} %broadcast_select_fusion.5), channel_id=1, replica_groups=mesh['samp'=32,'feat'=8] {'samp','feat'}, use_global_device_ids=true, to_apply=%region_11.12 | all-reduce | flops 128 | bytes 1024 | tf_op jit(solution)/shard_map/psum | solution.py:50
  699.7 1.1 multiply_subtract_fusion.3
  700.8 8.3 convolution_bitcast_fusion
  709.1 0.0 all-reduce.20.cloned.1.call-start
  709.1 139.2 %all-reduce.18.cloned.1.call-done = f32[2048,64]{0,1:T(8,128)} async-done(((f32[2048,64]{0,1:T(8,128)}), f32[2048,64]{0,1:T(8,128)}) %all-reduce.18.cloned.1.call-update) | async-done | bytes 524304 | tf_op jit(solution)/shard_map/psum | solution.py:29
  848.3 1.3 multiply_reduce_fusion.1
  849.7 78.9 %psum.111 = f32[64]{0:T(128)S(1)} all-reduce(f32[64]{0:T(128)S(1)} %broadcast_select_fusion.4), channel_id=1, replica_groups=mesh['samp'=32,'feat'=8] {'samp','feat'}, use_global_device_ids=true, to_apply=%region_16.17 | all-reduce | flops 64 | bytes 512 | tf_op jit(solution)/shard_map/psum | solution.py:34
  928.6 1.4 multiply_reduce_fusion
  930.0 11.1 %convolution_bitcast_fusion.2 = f32[1024,64]{0,1:T(8,128)} fusion(f32[2048,64]{0,1:T(8,128)S(1)} %get-tuple-element.9, f32[1024,2048]{1,0:T(8,128)} %param.3), kind=kOutput, calls=%fused_computation.2 | convolution fusion | flops 1610612736 | bytes 9175040 | tf_op jit(solution)/shard_map/dot_general | solution.py:43
  941.1 58.4 %all-reduce.20.cloned.1.call-done = f32[1024,64]{0,1:T(8,128)} async-done(((f32[1024,64]{0,1:T(8,128)}), f32[1024,64]{0,1:T(8,128)}) %all-reduce.20.cloned.1.call-update) | async-done | bytes 262160 | tf_op jit(solution)/shard_map/psum | solution.py:46
  999.5 1.1 multiply_reduce_fusion.5
  1000.5 78.4 %all-reduce = (f32[64]{0:T(128)S(1)}, f32[64]{0:T(128)S(1)}) all-reduce(f32[64]{0:T(128)S(1)} %broadcast_select_fusion, f32[64]{0:T(128)S(1)} %broadcast_select_fusion.3), channel_id=1, replica_groups=mesh['samp'=32,'feat'=8] {'samp','feat'}, use_global_device_ids=true, to_apply=%region_19.20 | all-reduce | flops 128 | bytes 1024 | tf_op jit(solution)/shard_map/psum | solution.py:50
  1078.9 1.7 multiply_subtract_fusion.2
  1080.7 1.0 multiply_add_fusion
  (29 shorter events, 0.3 us)
Async XLA Ops:
  7.2 313.0 %copy-start.1 = (f32[1024,64]{0,1:T(8,128)S(1)}, f32[1024,64]{0,1:T(8,128)}, u32[]{:S(2)}) copy-start(f32[1024,64]{0,1:T(8,128)} %param.4) | copy-start | bytes 786436
  7.2 313.0 %copy-start.3 = (f32[64]{0:T(128)S(1)}, f32[64]{0:T(128)}, u32[]{:S(2)}) copy-start(f32[64]{0:T(128)} %param.5) | copy-start | bytes 772
  7.2 156.4 %all-reduce.10.cloned.1.call-start = ((), (), s32[]{:S(2)}) async-start(), calls=%async_computation | async-start | bytes 1048576 | tf_op jit(solution)/shard_map/psum | solution.py:29
  16.8 223.7 %all-reduce.12.cloned.1.call-start = ((), (), s32[]{:S(2)}) async-start(), calls=%async_computation.1 | async-start | bytes 524288 | tf_op jit(solution)/shard_map/psum | solution.py:46
  163.6 12.4 %copy-start = (f32[2048,64]{0,1:T(8,128)S(1)}, f32[2048,64]{0,1:T(8,128)}, u32[]{:S(2)}) copy-start(f32[2048,64]{0,1:T(8,128)} %all-reduce.10.cloned.1.call-done) | copy-start | bytes 1572868
  175.9 293.0 %all-reduce.14.cloned.1.call-start = ((), (), s32[]{:S(2)}) async-start(), calls=%async_computation.2 | async-start | bytes 1048576 | tf_op jit(solution)/shard_map/psum | solution.py:29
  329.6 370.1 %copy-start.2 = (f32[1024,64]{0,1:T(8,128)S(1)}, f32[1024,64]{0,1:T(8,128)}, u32[]{:S(2)}) copy-start(f32[1024,64]{0,1:T(8,128)} %all-reduce.12.cloned.1.call-done) | copy-start | bytes 786436
  329.6 290.4 %all-reduce.16.cloned.1.call-start = ((), (), s32[]{:S(2)}) async-start(), calls=%async_computation.3 | async-start | bytes 524288 | tf_op jit(solution)/shard_map/psum | solution.py:46
  561.6 286.6 %all-reduce.18.cloned.1.call-start = ((), (), s32[]{:S(2)}) async-start(), calls=%async_computation.4 | async-start | bytes 1048576 | tf_op jit(solution)/shard_map/psum | solution.py:29
  709.1 290.4 %all-reduce.20.cloned.1.call-start = ((), (), s32[]{:S(2)}) async-start(), calls=%async_computation.5 | async-start | bytes 524288 | tf_op jit(solution)/shard_map/psum | solution.py:46
Sparse Core Ops, SparseCore 0:
  17.0 146.5 all-reduce.9
  176.1 64.4 all-reduce.11
  329.7 139.1 all-reduce.13
  561.8 58.2 all-reduce.15
  709.2 139.0 all-reduce.17
  941.2 58.2 all-reduce.19
where the time goes:
time: 1090 us
  waiting for transfers between devices  606 us (56%)
  blocking collectives  393 us (36%)
  matrix products  61.8 us (6%)
  between operations  14.2 us (1%)
  other arithmetic  12.6 us (1%)
    psum x3, waiting for transfers between devices, gradient_of(): return lax.psum(transposed(residual_full), 'samp')  425 us
    psum x3, blocking collectives, gradient_sq(): return lax.psum(local, ('samp', 'feat'))  236 us
    psum x3, waiting for transfers between devices, per_device(): image = lax.psum(partial_value, 'feat')  181 us
    psum x2, blocking collectives, per_device(): total_image, total_dir = lax.psum((image_sq, dir_sq), ('samp', 'feat'))  157 us
    dot_general x3, matrix products, per_device(): jnp.dot(features, full_dir, precision=high, preferred_element_type=jnp.fl...  34.5 us
    dot_general x3, matrix products, transposed(): lax.dot_general(features, residual_full, (((0,), (0,)), ((), ())), precis...  27.3 us
  transfers between devices with their start and end apart: 6, of which 6 were waited for; matrix products, arithmetic and copies ran while one was open for 0% of the time, Pallas kernels for 0%

commit v1 on v0

v1 whole, which is shorter than its diff:
```python
import functools

import jax
import jax.numpy as jnp
from jax import lax
from jax.experimental import pallas as pl
from jax.experimental.pallas import tpu as pltpu
from jax.sharding import PartitionSpec as P

NZ, NX, NY, NC = 8, 4, 4, 2
Y_SHIFTS = [[(i, (i + NC * k) % (NY * NC)) for i in range(NY * NC)] for k in (3, 1, 2)]
X_SHIFTS = [[(i, i // NX * NX + (i + k) % NX) for i in range(NZ * NX)] for k in range(NX)]
GROUPS_Z = [[z * NX + x for z in range(NZ)] for x in range(NX)]
CORE_SWAP = [(i, i ^ 1) for i in range(NY * NC)]

T = 64
F = 2048
S = 1024
H = S // 2
N = NZ * NX
TB, FB = T // NZ, F // NX
TILES = (T // 8) * (H // 128)

f32, bf16 = jnp.float32, jnp.bfloat16
QUARTER = ((T // 8 * FB // 128, 8, 128), f32)
LINE = FB // 128
HALF = ((TILES + 1, 8, 128), f32)
TINY = 1e-35
VMEM = pl.BlockSpec(memory_space=pltpu.VMEM)
NN = (((1,), (0,)), ((), ()))
PIECES = 4
PIECE = S // PIECES


def call(kernel, outs, name, mib=10):
    shapes = [pltpu.VMEM(shape, dtype) for shape, dtype in outs]
    def run(*args):
        return pl.pallas_call(
            kernel,
            in_specs=[VMEM] * len(args),
            out_specs=[VMEM] * len(shapes),
            out_shape=shapes,
            compiler_params=pltpu.CompilerParams(vmem_limit_bytes=mib * 2**20),
            name=name,
        )(*args)
    return run


def split(value):
    high = value.astype(bf16)
    return high, (value - high.astype(f32)).astype(bf16)


def product(both, high, a_high, a_low):
    first = lax.dot_general(both, a_high, NN, preferred_element_type=f32)
    second = lax.dot_general(high, a_low, NN, preferred_element_type=f32)
    return first[:T] + first[T:] + second


def block_in(ref, z):
    return jnp.concatenate([ref[z * LINE + j] for j in range(LINE)], axis=1)


def half_in(ref):
    lines = [[ref[i * (H // 128) + j] for j in range(H // 128)] for i in range(T // 8)]
    return jnp.concatenate([jnp.concatenate(line, axis=1) for line in lines], axis=0)


def put_half(ref, value):
    for i in range(T // 8):
        for j in range(H // 128):
            ref[i * (H // 128) + j] = value[8 * i : 8 * i + 8, 128 * j : 128 * j + 128]


def wide(ref):
    rows = [jnp.concatenate([ref[z * NX + x] for x in range(NX)], axis=1) for z in range(NZ)]
    return jnp.concatenate(rows, axis=0)


def quarter(shift):
    at = (lax.axis_index("samp") + shift) % NX
    return at, pl.ds(pl.multiple_of(at * FB, FB), FB)


def row_of(value):
    total = value[:, :128]
    for at in range(128, value.shape[1], 128):
        total = total + value[:, at : at + 128]
    return jnp.sum(total.T, axis=0, keepdims=True)


def rows_tile(rows):
    tile = jnp.concatenate(rows + [jnp.zeros((8 - len(rows), T), f32)], axis=0)
    return jnp.concatenate([tile, jnp.zeros((8, 128 - T), f32)], axis=1)


def columns_of(tile, count):
    turned = tile.T
    return [turned[:T, i : i + 1] for i in range(count)]


def scale0(tile):
    (square,) = columns_of(tile, 1)
    return lax.rsqrt(jnp.maximum(square, TINY))


def scale1(tile):
    overlap, square = columns_of(tile, 2)
    left = jnp.maximum(square - overlap * overlap, 1e-6 * square)
    return overlap, lax.rsqrt(jnp.maximum(left, TINY))


def tile_in(own_ref):
    return own_ref[TILES]


def first_kernel(a_hbm, b_hbm, out_ref, both_ref, high_ref, low_ref, a_ref, b_ref, sems):
    copies = [pltpu.make_async_copy(b_hbm, b_ref, sems.at[PIECES])]
    for i in range(PIECES):
        rows = pl.ds(i * PIECE, PIECE)
        copies.append(pltpu.make_async_copy(a_hbm.at[rows, :], a_ref.at[i], sems.at[i]))
    for copy in copies:
        copy.start()
    copies[0].wait()
    high, low = split(b_ref[...])
    both = jnp.concatenate([high, low], axis=0)
    for i in range(PIECES):
        copies[i + 1].wait()
        a_high, a_low = split(a_ref[i])
        rows = slice(i * PIECE, (i + 1) * PIECE)
        high_ref[rows, :] = a_high
        low_ref[rows, :] = a_low
    both_ref[...] = both
    _, at = quarter(2)
    put_half(out_ref, product(both, high, high_ref[:, at], low_ref[:, at]))


def first_more_kernel(shift, both_ref, high_ref, low_ref, out_ref):
    both = both_ref[...]
    _, at = quarter(shift)
    put_half(out_ref, product(both, both[:T], high_ref[:, at], low_ref[:, at]))


def first_last_kernel(both_ref, high_ref, low_ref, out_ref, high_t_ref, low_t_ref):
    first_more_kernel(0, both_ref, high_ref, low_ref, out_ref)
    for rows in (slice(i, i + PIECE) for i in range(0, S, PIECE)):
        for columns in (slice(i, i + PIECE) for i in range(0, F, PIECE)):
            high_t_ref[columns, rows] = high_ref[rows, columns].T
            low_t_ref[columns, rows] = low_ref[rows, columns].T


def first(a, b_t):
    anywhere = pl.BlockSpec(memory_space=pltpu.HBM)
    a = pltpu.with_memory_space_constraint(a, pltpu.HBM)
    b_t = pltpu.with_memory_space_constraint(b_t, pltpu.HBM)
    return pl.pallas_call(
        first_kernel,
        in_specs=[anywhere, anywhere],
        out_specs=[VMEM] * 4,
        out_shape=[
            pltpu.VMEM(*QUARTER),
            pltpu.VMEM((2 * T, S), bf16),
            pltpu.VMEM((S, F), bf16),
            pltpu.VMEM((S, F), bf16),
        ],
        scratch_shapes=[
            pltpu.VMEM((PIECES, PIECE, F), f32),
            pltpu.VMEM((T, S), f32),
            pltpu.SemaphoreType.DMA((PIECES + 1,)),
        ],
        compiler_params=pltpu.CompilerParams(vmem_limit_bytes=16 * 2**20),
        name="first",
    )(a, b_t)


def add_kernel(*refs):
    total = refs[0][...]
    for ref in refs[1:-1]:
        total = total + ref[...]
    refs[-1][...] = total


def lines_kernel(*refs):
    out_ref = refs[-1]
    for z in range(NZ):
        for j in range(out_ref.shape[1]):
            at = z * LINE + j if j < LINE else NZ * LINE
            total = refs[0][at]
            for ref in refs[1:-1]:
                total = total + ref[at]
            out_ref[z, j] = total


def sum_lines_kernel(in_ref, out_ref, *tile_refs):
    total = in_ref[0]
    for z in range(1, NZ):
        total = total + in_ref[z]
    block = jnp.concatenate([total[j] for j in range(LINE)], axis=1)
    for i in range(N):
        out_ref[i] = block
    for tile_ref in tile_refs:
        tile_ref[...] = total[LINE]


def sum_over_samp(parts):
    tiles = parts[0].shape[0] - NZ * LINE
    got = [lax.ppermute(parts[k], "samp", X_SHIFTS[k]) for k in (3, 1, 2)]
    (part,) = call(lines_kernel, [((NZ, LINE + tiles, 8, 128), f32)], "sum_x")(parts[0], *got)
    got = lax.all_to_all(part, "samp", 0, 0, axis_index_groups=GROUPS_Z)
    outs = [((N, TB, FB), f32)] + [((8, 128), f32)] * tiles
    part, *tile = call(sum_lines_kernel, outs, "sum_z")(got)
    return lax.all_to_all(part, "samp", 0, 0), *tile


def half_rows(own):
    core = lax.axis_index("feat") % NC
    at = core if own else 1 - core
    return pl.ds(pl.multiple_of(at * H, H), H)


def forward_send(value, scalars, high_ref, low_ref, send_ref, both_ref):
    high, low = split(value)
    both = jnp.concatenate([high, low], axis=0)
    both_ref[...] = both
    at = half_rows(False)
    put_half(send_ref, product(both, high, high_ref[:, at], low_ref[:, at]))
    send_ref[TILES] = rows_tile(scalars)


def send0_kernel(g_ref, high_ref, low_ref, send_ref, both_ref):
    g = wide(g_ref)
    forward_send(g, [row_of(g * g)], high_ref, low_ref, send_ref, both_ref)


def send1_kernel(g_ref, own0_ref, w_ref, high_ref, low_ref, send_ref, both_ref):
    e0 = wide(g_ref) * scale0(tile_in(own0_ref))
    w = wide(w_ref)
    forward_send(w, [row_of(e0 * w), row_of(w * w)], high_ref, low_ref, send_ref, both_ref)


def basis01(g_ref, own0_ref, w1_ref, own1_ref):
    e0 = wide(g_ref) * scale0(tile_in(own0_ref))
    overlap, scale = scale1(tile_in(own1_ref))
    return e0, (wide(w1_ref) - overlap * e0) * scale


def send2_kernel(
    g_ref, own0_ref, w1_ref, own1_ref, w_ref, tile_ref, high_ref, low_ref, send_ref, both_ref, q_ref
):
    e0, e1 = basis01(g_ref, own0_ref, w1_ref, own1_ref)
    overlap0, overlap1 = columns_of(tile_ref[...], 2)
    q = wide(w_ref) - overlap0 * e0 - overlap1 * e1
    q_ref[...] = q
    pairs = [(e0, e0), (e0, e1), (e0, q), (e1, e1), (e1, q), (q, q)]
    scalars = [row_of(p * q) for p, q in pairs]
    forward_send(q, scalars, high_ref, low_ref, send_ref, both_ref)


def keep_kernel(both_ref, send_ref, high_ref, low_ref, keep_ref):
    both = both_ref[...]
    at = half_rows(True)
    put_half(keep_ref, product(both, both[:T], high_ref[:, at], low_ref[:, at]))
    keep_ref[TILES] = send_ref[TILES]


def sum_over_feat(kernel, args, turned, name, extra=()):
    outs = [HALF, ((2 * T, F), bf16), *extra]
    send, both, *extra = call(kernel, outs, name)(*args, *turned)
    got = lax.ppermute(send, "feat", CORE_SWAP)
    (keep,) = call(keep_kernel, [HALF], "keep")(both, send, *turned)
    (part,) = call(add_kernel, [HALF], "add")(keep, got)
    got = [lax.ppermute(part, "feat", shift) for shift in Y_SHIFTS]
    (own,) = call(add_kernel, [HALF], "sum_y")(part, *got)
    return own, lax.ppermute(own, "feat", CORE_SWAP), *extra


def image0(tile_ref, half0_ref):
    return half_in(half0_ref) * scale0(tile_in(tile_ref))


def image1(tile0_ref, half0_ref, tile1_ref, half1_ref):
    overlap, scale = scale1(tile_in(tile1_ref))
    return (half_in(half1_ref) - overlap * image0(tile0_ref, half0_ref)) * scale


def back_own(value, high_ref, low_ref, out_ref):
    high, low = split(value)
    both = jnp.concatenate([high, low], axis=0)
    rows = half_rows(True)
    for x in range(NX):
        at = slice(x * FB, (x + 1) * FB)
        out_ref[x] = product(both, high, high_ref[rows, at], low_ref[rows, at])


def ready(value, both_ref):
    high, low = split(value)
    both_ref[...] = jnp.concatenate([high, low], axis=0)


def back_other_kernel(shift, both_ref, acc_ref, high_ref, low_ref, *refs):
    both = both_ref[...]
    rows = half_rows(False)
    place, at = quarter(shift)
    out_ref = refs[-1]
    put_half(out_ref, acc_ref[place] + product(both, both[:T], high_ref[rows, at], low_ref[rows, at]))
    for tile_ref in refs[:-1]:
        out_ref[NZ * LINE] = tile_ref[...]


def back0_own_kernel(own0_ref, high_ref, low_ref, out_ref):
    back_own(image0(own0_ref, own0_ref), high_ref, low_ref, out_ref)


def back0_ready_kernel(own0_ref, other0_ref, both_ref):
    ready(image0(own0_ref, other0_ref), both_ref)


def overlaps(u0, u1):
    return rows_tile([row_of(u0 * u1), row_of(u1 * u1)])


def back1_own_kernel(own0_ref, own1_ref, high_ref, low_ref, out_ref, tile_ref):
    u1 = image1(own0_ref, own0_ref, own1_ref, own1_ref)
    back_own(u1, high_ref, low_ref, out_ref)
    tile_ref[...] = overlaps(image0(own0_ref, own0_ref), u1)


def back1_ready_kernel(own0_ref, other0_ref, own1_ref, other1_ref, tile_ref, both_ref, out_tile_ref):
    u1 = image1(own0_ref, other0_ref, own1_ref, other1_ref)
    ready(u1, both_ref)
    out_tile_ref[...] = tile_ref[...] + overlaps(image0(own0_ref, other0_ref), u1)


def transposed(own_kernel, ready_kernel, owns, halves, a_high, a_low, tiles, name):
    tile = [((8, 128), f32)] * tiles
    outs = [((NX, T, FB), f32)] + tile
    acc, *scalars = call(own_kernel, outs, name + "_own")(*owns, a_high, a_low)
    outs = [((2 * T, H), bf16)] + tile
    both, *scalars = call(ready_kernel, outs, name + "_ready")(*halves, *scalars)
    parts = [None] * NX
    (count, *rest), dtype = QUARTER
    for k in (2, 1, 3, 0):
        kernel = functools.partial(back_other_kernel, k)
        outs = [((count + tiles, *rest), dtype)]
        (parts[k],) = call(kernel, outs, name + "_other")(both, acc, a_high, a_low, *scalars)
    return parts


PAIRS = [(0, 0), (0, 1), (0, 2), (1, 1), (1, 2), (2, 2)]


def images(own0_ref, own1_ref, own2_ref, half0_ref, half1_ref, half2_ref):
    u0 = image0(own0_ref, half0_ref)
    u1 = image1(own0_ref, half0_ref, own1_ref, half1_ref)
    square = columns_of(tile_in(own2_ref), 6)[5]
    return u0, u1, half_in(half2_ref) * lax.rsqrt(jnp.maximum(square, TINY))


def gram_rows(*refs):
    u = images(*refs)
    return rows_tile([row_of(u[i] * u[j]) for i, j in PAIRS])


def gram_own_kernel(own0_ref, own1_ref, own2_ref, out_ref):
    out_ref[...] = gram_rows(own0_ref, own1_ref, own2_ref, own0_ref, own1_ref, own2_ref)


def gram_kernel(own0_ref, other0_ref, own1_ref, other1_ref, own2_ref, other2_ref, tile_ref, out_ref):
    tile = tile_ref[...]
    tile += gram_rows(own0_ref, own1_ref, own2_ref, other0_ref, other1_ref, other2_ref)
    for i in range(out_ref.shape[0]):
        out_ref[i] = tile


def solve(gram, dots, square0, ridge):
    scale2 = lax.rsqrt(jnp.maximum(dots[5], TINY))
    e = [dots[0], dots[1], dots[2] * scale2, dots[3], dots[4] * scale2, dots[5] * scale2 * scale2]
    k00, k01, k02, k11, k12, k22 = [u + ridge * v for u, v in zip(gram, e)]
    norm = jnp.sqrt(square0)
    r0, r1, r2 = e[0] * norm, e[1] * norm, e[2] * norm
    inverse0 = 1.0 / jnp.maximum(k00, TINY)
    l10, l20 = k01 * inverse0, k02 * inverse0
    d1 = k11 - l10 * k01
    inverse1 = jnp.where(d1 > 1e-6 * k11, 1.0 / jnp.maximum(d1, TINY), 0.0)
    t = k12 - l20 * k01
    l21 = t * inverse1
    d2 = k22 - l20 * k02 - l21 * t
    inverse2 = jnp.where(d2 > 1e-6 * k22, 1.0 / jnp.maximum(d2, TINY), 0.0)
    z1 = r1 - l10 * r0
    z2 = r2 - l20 * r0 - l21 * z1
    c2 = z2 * inverse2
    c1 = z1 * inverse1 - l21 * c2
    c0 = r0 * inverse0 - l10 * c1 - l20 * c2
    return c0, c1, c2, c2 * scale2


def last_kernel(
    gram_ref, ridge_ref, b_ref, g_ref, w1_ref, q_ref,
    own0_ref, other0_ref, own1_ref, other1_ref, own2_ref, other2_ref, x_ref, r_ref,
):
    gram = gram_ref[0]
    for i in range(1, gram_ref.shape[0]):
        gram = gram + gram_ref[i]
    dots = tile_in(own2_ref)
    row = lambda tile, i: tile[i : i + 1, :]
    coefficients = solve(
        [row(gram, i) for i in range(6)],
        [row(dots, i) for i in range(6)],
        row(tile_in(own0_ref), 0),
        jnp.concatenate([ridge_ref[...], jnp.zeros((1, 128 - T), f32)], axis=1),
    )
    tile = jnp.concatenate(list(coefficients) + [jnp.zeros((4, 128), f32)], axis=0)
    c0, c1, _, c2 = columns_of(tile, 4)
    e0, e1 = basis01(g_ref, own0_ref, w1_ref, own1_ref)
    x_ref[...] = c0 * e0 + c1 * e1 + c2 * q_ref[...]
    for own, half0_ref, half1_ref, half2_ref in (
        (True, own0_ref, own1_ref, own2_ref),
        (False, other0_ref, other1_ref, other2_ref),
    ):
        u0 = image0(own0_ref, half0_ref)
        u1 = image1(own0_ref, half0_ref, own1_ref, half1_ref)
        at = half_rows(own)
        r_ref[:, at] = b_ref[:, at] - c0 * u0 - c1 * u1 - c2 * half_in(half2_ref)


def last(*args):
    return pl.pallas_call(
        last_kernel,
        in_specs=[VMEM] * len(args),
        out_specs=[VMEM, VMEM],
        out_shape=[jax.ShapeDtypeStruct((T, F), f32), jax.ShapeDtypeStruct((T, S), f32)],
        compiler_params=pltpu.CompilerParams(vmem_limit_bytes=16 * 2**20),
        name="last",
    )(*args)


def per_device(features, targets, ridge):
    b_t = targets.T
    parts = {}
    parts[2], both, a_high, a_low = first(features, b_t)
    for k in (1, 3):
        kernel = functools.partial(first_more_kernel, k)
        (parts[k],) = call(kernel, [QUARTER], "first_more")(both, a_high, a_low)
    outs = [QUARTER, ((F, S), bf16), ((F, S), bf16)]
    parts[0], *turned = call(first_last_kernel, outs, "first_last")(both, a_high, a_low)
    (g,) = sum_over_samp(parts)
    own0, other0 = sum_over_feat(send0_kernel, (g,), turned, "send0")
    parts = transposed(
        back0_own_kernel, back0_ready_kernel, (own0,), (own0, other0), a_high, a_low, 0, "back0"
    )
    (w1,) = sum_over_samp(parts)
    own1, other1 = sum_over_feat(send1_kernel, (g, own0, w1), turned, "send1")
    halves = (own0, other0, own1, other1)
    parts = transposed(
        back1_own_kernel, back1_ready_kernel, (own0, own1), halves, a_high, a_low, 1, "back1"
    )
    w2, tile = sum_over_samp(parts)
    args = (g, own0, w1, own1, w2, tile)
    own2, other2, q = sum_over_feat(send2_kernel, args, turned, "send2", [((T, F), f32)])
    halves = (own0, other0, own1, other1, own2, other2)
    (tile,) = call(gram_own_kernel, [((8, 128), f32)], "gram_own")(own0, own1, own2)
    (tiles,) = call(gram_kernel, [((N, 8, 128), f32)], "gram")(*halves, tile)
    gram = lax.all_to_all(tiles, "samp", 0, 0)
    x, r = last(gram, ridge.reshape(1, T), b_t, g, w1, q, *halves)
    return x.T, r.T


def solution(mesh):
    placed = (P("samp", "feat"), P("samp", None), P())
    return jax.shard_map(
        per_device,
        mesh=mesh,
        in_specs=placed,
        out_specs=(P("feat", None), P("samp", None)),
        check_vma=False,
    )
```

time: 1090 us -> 200 us (0.18)
  waiting for transfers between devices: 606 us -> 30.6 us
  blocking collectives: 393 us -> 99.7 us
  matrix products: 61.8 us -> 0 us
  starting transfers between devices: 0.25 us -> 46.7 us
  Pallas kernels: 0 us -> 21.2 us
  between operations: 14.2 us -> 0.89 us
  other arithmetic: 12.6 us -> 0 us
    psum x6 -> x0, waiting for transfers between devices: 606 us -> none  [the longest x3 425 us: gradient_of(): return lax.psum(transposed(residual_full), 'samp')]
    psum x5 -> x0, blocking collectives: 393 us -> none  [the longest x3 236 us: gradient_sq(): return lax.psum(local, ('samp', 'feat'))]
    all_to_all x0 -> x7, blocking collectives: none -> 99.7 us  [the longest x3 49.1 us: sum_over_samp(): return (lax.all_to_all(part, 'samp', 0, 0), *tile)]
    dot_general x6 -> x0, matrix products: 61.8 us -> none  [the longest x3 34.5 us: per_device(): jnp.dot(features, full_dir, precision=high, preferred_element_type=jnp.fl...]
    ppermute x0 -> x24, starting transfers between devices: none -> 46.7 us  [the longest x3 17.6 us: sum_over_feat(): got = lax.ppermute(send, 'feat', CORE_SWAP)]
    ppermute x0 -> x24, waiting for transfers between devices: none -> 30.6 us  [the longest x9 15 us: sum_over_feat(): got = [lax.ppermute(part, 'feat', shift) for shift in Y_SHIFTS]]
    pallas_call x0 -> x37, Pallas kernels: none -> 21.2 us  [the longest x35 15.2 us: run(): pl.pallas_call(kernel, in_specs=[VMEM] * len(args), out_specs=[VMEM] * le...]
  transfers between devices with their start and end apart: 6 -> 24, of which waited for: 6 -> 17; matrix products, arithmetic and copies ran while one was open for 0% -> 0% of each run, Pallas kernels for 0% -> 4%
where the time goes in v1:
time: 200 us; the launch traced here: 199 us
  blocking collectives  99.7 us (50%)
  starting transfers between devices  46.7 us (23%)
  waiting for transfers between devices  30.6 us (15%)
  Pallas kernels  21.2 us (11%)
    all_to_all x3, blocking collectives, sum_over_samp(): return (lax.all_to_all(part, 'samp', 0, 0), *tile)  49.1 us
    all_to_all x3, blocking collectives, sum_over_samp(): got = lax.all_to_all(part, 'samp', 0, 0, axis_index_groups=GROUPS_Z)  37.5 us
    ppermute x3, starting transfers between devices, sum_over_feat(): got = lax.ppermute(send, 'feat', CORE_SWAP)  17.6 us
    pallas_call x35, Pallas kernels, run(): pl.pallas_call(kernel, in_specs=[VMEM] * len(args), out_specs=[VMEM] * le...  15.2 us
    ppermute x9, waiting for transfers between devices, sum_over_feat(): got = [lax.ppermute(part, 'feat', shift) for shift in Y_SHIFTS]  15 us
    ppermute x9, starting transfers between devices, sum_over_feat(): got = [lax.ppermute(part, 'feat', shift) for shift in Y_SHIFTS]  14.5 us
    ppermute x9, waiting for transfers between devices, sum_over_samp(): got = [lax.ppermute(parts[k], 'samp', X_SHIFTS[k]) for k in (3, 1, 2)]  14.4 us
    all_to_all x1, blocking collectives, per_device(): gram = lax.all_to_all(tiles, 'samp', 0, 0)  13.1 us
  transfers between devices with their start and end apart: 24, of which 17 were waited for; matrix products, arithmetic and copies ran while one was open for 0% of the time, Pallas kernels for 4%

profile of v1, /device:TPU:1, one launch (start us, length us, event | category | flops | bytes accessed | tf_op | source)
XLA Modules:
  0.0 199.1 jit_solution(5042212961513188009)
XLA Ops:
  0.6 4.6 %first.1 = (f32[32,8,128]{2,1,0:T(8,128)S(1)}, bf16[128,1024]{1,0:T(8,128)(2,1)S(1)}, bf16[1024,2048]{1,0:T(8,128)(2,1)S(1)}, bf16[1024,2048]{1,0:T(8,128)(2,1)S(1)}) custom-call(f32[1024,2048]{1,0:T(8,128)} %a_hbm.1, f32[64,1024]{1,0:T(8,128)} %bitcast.4), custom_call_target="tpu_custom_call" | custom-call | tf_op jit(solution)/shard_map/first/pallas_call | solution.py:156
  5.7 3.4 %collective-permute-start = (f32[32,8,128]{2,1,0:T(8,128)S(1)}, f32[32,8,128]{2,1,0:T(8,128)S(1)}, u32[]{:S(2)}, u32[]{:S(2)}) collective-permute-start(f32[32,8,128]{2,1,0:T(8,128)S(1)} %first_more.2), channel_id=1, source_target_pairs={{0,24},{8,0},{16,8},{24,16},{32,56},{40,32},{48,40},{56,48},{64,88... | collective-permute-start | bytes 393224 | tf_op jit(solution)/shard_map/ppermute | solution.py:207
  9.7 1.7 collective-permute-start.2
  11.3 2.5 %first_last.1 = (f32[32,8,128]{2,1,0:T(8,128)S(1)}, bf16[2048,1024]{1,0:T(8,128)(2,1)S(1)}, bf16[2048,1024]{1,0:T(8,128)(2,1)S(1)}) custom-call(bf16[128,1024]{1,0:T(8,128)(2,1)S(1)} %get-tuple-element.24.both_ref, bf16[1024,2048]{1,0:T(8,128)(2,1)S(1)} %get-tuple-element.25.high_ref, bf16[1024,2048]{1,0:T(8,128)(2,1)S(1)} %get-tuple-element.26.low_ref), custom_call_target="tpu_custom_call" | custom-call | tf_op jit(solution)/shard_map/first_last/pallas_call | solution.py:38
  13.8 3.2 %collective-permute-done.1.refs_2_ = f32[32,8,128]{2,1,0:T(8,128)S(1)} collective-permute-done((f32[32,8,128]{2,1,0:T(8,128)S(1)}, f32[32,8,128]{2,1,0:T(8,128)S(1)}, u32[]{:S(2)}, u32[]{:S(2)}) %collective-permute-start.1) | collective-permute-done | bytes 131104 | tf_op jit(solution)/shard_map/ppermute | solution.py:207
  17.1 15.8 %all_to_all.35.in_ref = f32[8,4,8,128]{3,2,1,0:T(8,128)S(1)} all-to-all(f32[8,4,8,128]{3,2,1,0:T(8,128)S(1)} %sum_x.3), channel_id=1, replica_groups={{0,32,64,96,128,160,192,224},{8,40,72,104,136,168,200,232},{16,48,80,11..., dimensions={0} | all-to-all | bytes 262144 | tf_op jit(solution)/shard_map/all_to_all | solution.py:209
  32.9 16.1 %all_to_all.36.g_ref = f32[32,8,512]{2,1,0:T(8,128)S(1)} all-to-all(f32[32,8,512]{2,1,0:T(8,128)S(1)} %sum_z.3), channel_id=1, replica_groups=mesh['samp'=32,'feat'=8] {'samp'}, dimensions={0} | all-to-all | bytes 1048576 | tf_op jit(solution)/shard_map/all_to_all | solution.py:212
  49.8 6.2 %collective-permute-start.3 = (f32[33,8,128]{2,1,0:T(8,128)S(1)}, f32[33,8,128]{2,1,0:T(8,128)S(1)}, u32[]{:S(2)}, u32[]{:S(2)}) collective-permute-start(f32[33,8,128]{2,1,0:T(8,128)S(1)} %get-tuple-element.32.send_ref), channel_id=1, source_target_pairs={{0,1},{1,0},{2,3},{3,2},{4,5},{5,4},{6,7},{7,6},{8,9},{9,8},{10,11... | collective-permute-start | bytes 405512 | tf_op jit(solution)/shard_map/ppermute | solution.py:269
  57.0 3.0 %collective-permute-start.6 = (f32[33,8,128]{2,1,0:T(8,128)S(1)}, f32[33,8,128]{2,1,0:T(8,128)S(1)}, u32[]{:S(2)}, u32[]{:S(2)}) collective-permute-start(f32[33,8,128]{2,1,0:T(8,128)S(1)} %add.3.refs_0_), channel_id=1, source_target_pairs={{0,4},{1,5},{2,6},{3,7},{4,0},{5,1},{6,2},{7,3},{8,12},{9,13},{10,... | collective-permute-start | bytes 405512 | tf_op jit(solution)/shard_map/ppermute | solution.py:272
  60.4 2.3 %collective-permute-start.4 = (f32[33,8,128]{2,1,0:T(8,128)S(1)}, f32[33,8,128]{2,1,0:T(8,128)S(1)}, u32[]{:S(2)}, u32[]{:S(2)}) collective-permute-start(f32[33,8,128]{2,1,0:T(8,128)S(1)} %add.3.refs_0_), channel_id=1, source_target_pairs={{0,6},{1,7},{2,0},{3,1},{4,2},{5,3},{6,4},{7,5},{8,14},{9,15},{10,... | collective-permute-start | bytes 405512 | tf_op jit(solution)/shard_map/ppermute | solution.py:272
  63.4 3.4 %collective-permute-done.5.refs_2_ = f32[33,8,128]{2,1,0:T(8,128)S(1)} collective-permute-done((f32[33,8,128]{2,1,0:T(8,128)S(1)}, f32[33,8,128]{2,1,0:T(8,128)S(1)}, u32[]{:S(2)}, u32[]{:S(2)}) %collective-permute-start.5) | collective-permute-done | bytes 135200 | tf_op jit(solution)/shard_map/ppermute | solution.py:272
  70.3 1.6 collective-permute-start.8
  71.9 1.8 collective-permute-start.10
  75.1 3.6 %collective-permute-done.9.refs_2_ = f32[32,8,128]{2,1,0:T(8,128)S(1)} collective-permute-done((f32[32,8,128]{2,1,0:T(8,128)S(1)}, f32[32,8,128]{2,1,0:T(8,128)S(1)}, u32[]{:S(2)}, u32[]{:S(2)}) %collective-permute-start.9) | collective-permute-done | bytes 131104 | tf_op jit(solution)/shard_map/ppermute | solution.py:207
  79.4 10.7 %all_to_all.37.in_ref = f32[8,4,8,128]{3,2,1,0:T(8,128)S(1)} all-to-all(f32[8,4,8,128]{3,2,1,0:T(8,128)S(1)} %sum_x.4), channel_id=1, replica_groups={{0,32,64,96,128,160,192,224},{8,40,72,104,136,168,200,232},{16,48,80,11..., dimensions={0} | all-to-all | bytes 262144 | tf_op jit(solution)/shard_map/all_to_all | solution.py:209
  90.2 16.5 %all_to_all.38.w_ref.w1_ref = f32[32,8,512]{2,1,0:T(8,128)S(1)} all-to-all(f32[32,8,512]{2,1,0:T(8,128)S(1)} %sum_z.4), channel_id=1, replica_groups=mesh['samp'=32,'feat'=8] {'samp'}, dimensions={0} | all-to-all | bytes 1048576 | tf_op jit(solution)/shard_map/all_to_all | solution.py:212
  107.6 5.7 %collective-permute-start.11 = (f32[33,8,128]{2,1,0:T(8,128)S(1)}, f32[33,8,128]{2,1,0:T(8,128)S(1)}, u32[]{:S(2)}, u32[]{:S(2)}) collective-permute-start(f32[33,8,128]{2,1,0:T(8,128)S(1)} %get-tuple-element.34.send_ref), channel_id=1, source_target_pairs={{0,1},{1,0},{2,3},{3,2},{4,5},{5,4},{6,7},{7,6},{8,9},{9,8},{10,11... | collective-permute-start | bytes 405512 | tf_op jit(solution)/shard_map/ppermute | solution.py:269
  114.3 1.9 collective-permute-start.14
  118.8 1.9 collective-permute-done.14.refs_3_
  120.7 3.4 %collective-permute-done.13.refs_2_ = f32[33,8,128]{2,1,0:T(8,128)S(1)} collective-permute-done((f32[33,8,128]{2,1,0:T(8,128)S(1)}, f32[33,8,128]{2,1,0:T(8,128)S(1)}, u32[]{:S(2)}, u32[]{:S(2)}) %collective-permute-start.13) | collective-permute-done | bytes 135200 | tf_op jit(solution)/shard_map/ppermute | solution.py:272
  127.6 1.5 collective-permute-start.16
  129.1 1.7 collective-permute-start.18
  131.1 1.5 collective-permute-done.16.refs_1_
  132.6 3.2 %collective-permute-done.17.refs_2_ = f32[33,8,128]{2,1,0:T(8,128)S(1)} collective-permute-done((f32[33,8,128]{2,1,0:T(8,128)S(1)}, f32[33,8,128]{2,1,0:T(8,128)S(1)}, u32[]{:S(2)}, u32[]{:S(2)}) %collective-permute-start.17) | collective-permute-done | bytes 135200 | tf_op jit(solution)/shard_map/ppermute | solution.py:207
  136.9 11.0 %all_to_all.39.in_ref = f32[8,5,8,128]{3,2,1,0:T(8,128)S(1)} all-to-all(f32[8,5,8,128]{3,2,1,0:T(8,128)S(1)} %sum_x.5), channel_id=1, replica_groups={{0,32,64,96,128,160,192,224},{8,40,72,104,136,168,200,232},{16,48,80,11..., dimensions={0} | all-to-all | bytes 327680 | tf_op jit(solution)/shard_map/all_to_all | solution.py:209
  147.9 16.5 %all_to_all.40.w_ref = f32[32,8,512]{2,1,0:T(8,128)S(1)} all-to-all(f32[32,8,512]{2,1,0:T(8,128)S(1)} %get-tuple-element.39), channel_id=1, replica_groups=mesh['samp'=32,'feat'=8] {'samp'}, dimensions={0} | all-to-all | bytes 1048576 | tf_op jit(solution)/shard_map/all_to_all | solution.py:212
  165.8 5.7 %collective-permute-start.19 = (f32[33,8,128]{2,1,0:T(8,128)S(1)}, f32[33,8,128]{2,1,0:T(8,128)S(1)}, u32[]{:S(2)}, u32[]{:S(2)}) collective-permute-start(f32[33,8,128]{2,1,0:T(8,128)S(1)} %get-tuple-element.42.send_ref), channel_id=1, source_target_pairs={{0,1},{1,0},{2,3},{3,2},{4,5},{5,4},{6,7},{7,6},{8,9},{9,8},{10,11... | collective-permute-start | bytes 405512 | tf_op jit(solution)/shard_map/ppermute | solution.py:269
  172.5 1.6 collective-permute-start.22
  176.8 2.1 %collective-permute-done.22.refs_3_ = f32[33,8,128]{2,1,0:T(8,128)S(1)} collective-permute-done((f32[33,8,128]{2,1,0:T(8,128)S(1)}, f32[33,8,128]{2,1,0:T(8,128)S(1)}, u32[]{:S(2)}, u32[]{:S(2)}) %collective-permute-start.22) | collective-permute-done | bytes 135200 | tf_op jit(solution)/shard_map/ppermute | solution.py:272
  178.9 3.6 %collective-permute-done.21.refs_2_ = f32[33,8,128]{2,1,0:T(8,128)S(1)} collective-permute-done((f32[33,8,128]{2,1,0:T(8,128)S(1)}, f32[33,8,128]{2,1,0:T(8,128)S(1)}, u32[]{:S(2)}, u32[]{:S(2)}) %collective-permute-start.21) | collective-permute-done | bytes 135200 | tf_op jit(solution)/shard_map/ppermute | solution.py:272
  184.6 13.1 %all_to_all.41.gram_ref = f32[32,8,128]{2,1,0:T(8,128)S(1)} all-to-all(f32[32,8,128]{2,1,0:T(8,128)S(1)} %gram.1), channel_id=1, replica_groups=mesh['samp'=32,'feat'=8] {'samp'}, dimensions={0} | all-to-all | bytes 262144 | tf_op jit(solution)/shard_map/all_to_all | solution.py:463
  197.7 1.4 last.1
  (64 shorter events, 26.3 us)
Async XLA Ops:
  5.7 8.1 %collective-permute-start = (f32[32,8,128]{2,1,0:T(8,128)S(1)}, f32[32,8,128]{2,1,0:T(8,128)S(1)}, u32[]{:S(2)}, u32[]{:S(2)}) collective-permute-start(f32[32,8,128]{2,1,0:T(8,128)S(1)} %first_more.2), channel_id=1, source_target_pairs={{0,24},{8,0},{16,8},{24,16},{32,56},{40,32},{48,40},{56,48},{64,88... | collective-permute-start | bytes 393224 | tf_op jit(solution)/shard_map/ppermute | solution.py:207
  9.6 7.5 %collective-permute-start.1 = (f32[32,8,128]{2,1,0:T(8,128)S(1)}, f32[32,8,128]{2,1,0:T(8,128)S(1)}, u32[]{:S(2)}, u32[]{:S(2)}) collective-permute-start(f32[32,8,128]{2,1,0:T(8,128)S(1)} %first_more.3), channel_id=1, source_target_pairs={{0,8},{8,16},{16,24},{24,0},{32,40},{40,48},{48,56},{56,32},{64,72... | collective-permute-start | bytes 393224 | tf_op jit(solution)/shard_map/ppermute | solution.py:207
  9.7 7.4 %collective-permute-start.2 = (f32[32,8,128]{2,1,0:T(8,128)S(1)}, f32[32,8,128]{2,1,0:T(8,128)S(1)}, u32[]{:S(2)}, u32[]{:S(2)}) collective-permute-start(f32[32,8,128]{2,1,0:T(8,128)S(1)} %get-tuple-element.28), channel_id=1, source_target_pairs={{0,16},{8,24},{16,0},{24,8},{32,48},{40,56},{48,32},{56,40},{64,80... | collective-permute-start | bytes 393224 | tf_op jit(solution)/shard_map/ppermute | solution.py:207
  49.8 7.2 %collective-permute-start.3 = (f32[33,8,128]{2,1,0:T(8,128)S(1)}, f32[33,8,128]{2,1,0:T(8,128)S(1)}, u32[]{:S(2)}, u32[]{:S(2)}) collective-permute-start(f32[33,8,128]{2,1,0:T(8,128)S(1)} %get-tuple-element.32.send_ref), channel_id=1, source_target_pairs={{0,1},{1,0},{2,3},{3,2},{4,5},{5,4},{6,7},{7,6},{8,9},{9,8},{10,11... | collective-permute-start | bytes 405512 | tf_op jit(solution)/shard_map/ppermute | solution.py:269
  57.0 6.4 %collective-permute-start.6 = (f32[33,8,128]{2,1,0:T(8,128)S(1)}, f32[33,8,128]{2,1,0:T(8,128)S(1)}, u32[]{:S(2)}, u32[]{:S(2)}) collective-permute-start(f32[33,8,128]{2,1,0:T(8,128)S(1)} %add.3.refs_0_), channel_id=1, source_target_pairs={{0,4},{1,5},{2,6},{3,7},{4,0},{5,1},{6,2},{7,3},{8,12},{9,13},{10,... | collective-permute-start | bytes 405512 | tf_op jit(solution)/shard_map/ppermute | solution.py:272
  60.0 6.8 %collective-permute-start.5 = (f32[33,8,128]{2,1,0:T(8,128)S(1)}, f32[33,8,128]{2,1,0:T(8,128)S(1)}, u32[]{:S(2)}, u32[]{:S(2)}) collective-permute-start(f32[33,8,128]{2,1,0:T(8,128)S(1)} %add.3.refs_0_), channel_id=1, source_target_pairs={{0,2},{1,3},{2,4},{3,5},{4,6},{5,7},{6,0},{7,1},{8,10},{9,11},{10,... | collective-permute-start | bytes 405512 | tf_op jit(solution)/shard_map/ppermute | solution.py:272
  60.4 6.4 %collective-permute-start.4 = (f32[33,8,128]{2,1,0:T(8,128)S(1)}, f32[33,8,128]{2,1,0:T(8,128)S(1)}, u32[]{:S(2)}, u32[]{:S(2)}) collective-permute-start(f32[33,8,128]{2,1,0:T(8,128)S(1)} %add.3.refs_0_), channel_id=1, source_target_pairs={{0,6},{1,7},{2,0},{3,1},{4,2},{5,3},{6,4},{7,5},{8,14},{9,15},{10,... | collective-permute-start | bytes 405512 | tf_op jit(solution)/shard_map/ppermute | solution.py:272
  66.8 2.3 %collective-permute-start.7 = (f32[33,8,128]{2,1,0:T(8,128)S(1)}, f32[33,8,128]{2,1,0:T(8,128)S(1)}, u32[]{:S(2)}, u32[]{:S(2)}) collective-permute-start(f32[33,8,128]{2,1,0:T(8,128)S(1)} %sum_y.3.own0_ref), channel_id=1, source_target_pairs={{0,1},{1,0},{2,3},{3,2},{4,5},{5,4},{6,7},{7,6},{8,9},{9,8},{10,11... | collective-permute-start | bytes 405512 | tf_op jit(solution)/shard_map/ppermute | solution.py:274
  70.3 4.8 %collective-permute-start.8 = (f32[32,8,128]{2,1,0:T(8,128)S(1)}, f32[32,8,128]{2,1,0:T(8,128)S(1)}, u32[]{:S(2)}, u32[]{:S(2)}) collective-permute-start(f32[32,8,128]{2,1,0:T(8,128)S(1)} %back0_other.5), channel_id=1, source_target_pairs={{0,24},{8,0},{16,8},{24,16},{32,56},{40,32},{48,40},{56,48},{64,88... | collective-permute-start | bytes 393224 | tf_op jit(solution)/shard_map/ppermute | solution.py:207
  71.9 6.8 %collective-permute-start.9 = (f32[32,8,128]{2,1,0:T(8,128)S(1)}, f32[32,8,128]{2,1,0:T(8,128)S(1)}, u32[]{:S(2)}, u32[]{:S(2)}) collective-permute-start(f32[32,8,128]{2,1,0:T(8,128)S(1)} %back0_other.6), channel_id=1, source_target_pairs={{0,8},{8,16},{16,24},{24,0},{32,40},{40,48},{48,56},{56,32},{64,72... | collective-permute-start | bytes 393224 | tf_op jit(solution)/shard_map/ppermute | solution.py:207
  71.9 7.5 %collective-permute-start.10 = (f32[32,8,128]{2,1,0:T(8,128)S(1)}, f32[32,8,128]{2,1,0:T(8,128)S(1)}, u32[]{:S(2)}, u32[]{:S(2)}) collective-permute-start(f32[32,8,128]{2,1,0:T(8,128)S(1)} %back0_other.7), channel_id=1, source_target_pairs={{0,16},{8,24},{16,0},{24,8},{32,48},{40,56},{48,32},{56,40},{64,80... | collective-permute-start | bytes 393224 | tf_op jit(solution)/shard_map/ppermute | solution.py:207
  107.6 6.6 %collective-permute-start.11 = (f32[33,8,128]{2,1,0:T(8,128)S(1)}, f32[33,8,128]{2,1,0:T(8,128)S(1)}, u32[]{:S(2)}, u32[]{:S(2)}) collective-permute-start(f32[33,8,128]{2,1,0:T(8,128)S(1)} %get-tuple-element.34.send_ref), channel_id=1, source_target_pairs={{0,1},{1,0},{2,3},{3,2},{4,5},{5,4},{6,7},{7,6},{8,9},{9,8},{10,11... | collective-permute-start | bytes 405512 | tf_op jit(solution)/shard_map/ppermute | solution.py:269
  114.3 6.4 %collective-permute-start.14 = (f32[33,8,128]{2,1,0:T(8,128)S(1)}, f32[33,8,128]{2,1,0:T(8,128)S(1)}, u32[]{:S(2)}, u32[]{:S(2)}) collective-permute-start(f32[33,8,128]{2,1,0:T(8,128)S(1)} %add.4.refs_0_), channel_id=1, source_target_pairs={{0,4},{1,5},{2,6},{3,7},{4,0},{5,1},{6,2},{7,3},{8,12},{9,13},{10,... | collective-permute-start | bytes 405512 | tf_op jit(solution)/shard_map/ppermute | solution.py:272
  116.1 8.0 %collective-permute-start.13 = (f32[33,8,128]{2,1,0:T(8,128)S(1)}, f32[33,8,128]{2,1,0:T(8,128)S(1)}, u32[]{:S(2)}, u32[]{:S(2)}) collective-permute-start(f32[33,8,128]{2,1,0:T(8,128)S(1)} %add.4.refs_0_), channel_id=1, source_target_pairs={{0,2},{1,3},{2,4},{3,5},{4,6},{5,7},{6,0},{7,1},{8,10},{9,11},{10,... | collective-permute-start | bytes 405512 | tf_op jit(solution)/shard_map/ppermute | solution.py:272
  117.6 6.6 %collective-permute-start.12 = (f32[33,8,128]{2,1,0:T(8,128)S(1)}, f32[33,8,128]{2,1,0:T(8,128)S(1)}, u32[]{:S(2)}, u32[]{:S(2)}) collective-permute-start(f32[33,8,128]{2,1,0:T(8,128)S(1)} %add.4.refs_0_), channel_id=1, source_target_pairs={{0,6},{1,7},{2,0},{3,1},{4,2},{5,3},{6,4},{7,5},{8,14},{9,15},{10,... | collective-permute-start | bytes 405512 | tf_op jit(solution)/shard_map/ppermute | solution.py:272
  124.2 2.0 %collective-permute-start.15 = (f32[33,8,128]{2,1,0:T(8,128)S(1)}, f32[33,8,128]{2,1,0:T(8,128)S(1)}, u32[]{:S(2)}, u32[]{:S(2)}) collective-permute-start(f32[33,8,128]{2,1,0:T(8,128)S(1)} %sum_y.4.own1_ref), channel_id=1, source_target_pairs={{0,1},{1,0},{2,3},{3,2},{4,5},{5,4},{6,7},{7,6},{8,9},{9,8},{10,11... | collective-permute-start | bytes 405512 | tf_op jit(solution)/shard_map/ppermute | solution.py:274
  127.6 5.0 %collective-permute-start.16 = (f32[33,8,128]{2,1,0:T(8,128)S(1)}, f32[33,8,128]{2,1,0:T(8,128)S(1)}, u32[]{:S(2)}, u32[]{:S(2)}) collective-permute-start(f32[33,8,128]{2,1,0:T(8,128)S(1)} %back1_other.5), channel_id=1, source_target_pairs={{0,24},{8,0},{16,8},{24,16},{32,56},{40,32},{48,40},{56,48},{64,88... | collective-permute-start | bytes 405512 | tf_op jit(solution)/shard_map/ppermute | solution.py:207
  129.0 6.8 %collective-permute-start.17 = (f32[33,8,128]{2,1,0:T(8,128)S(1)}, f32[33,8,128]{2,1,0:T(8,128)S(1)}, u32[]{:S(2)}, u32[]{:S(2)}) collective-permute-start(f32[33,8,128]{2,1,0:T(8,128)S(1)} %back1_other.6), channel_id=1, source_target_pairs={{0,8},{8,16},{16,24},{24,0},{32,40},{40,48},{48,56},{56,32},{64,72... | collective-permute-start | bytes 405512 | tf_op jit(solution)/shard_map/ppermute | solution.py:207
  129.1 7.7 %collective-permute-start.18 = (f32[33,8,128]{2,1,0:T(8,128)S(1)}, f32[33,8,128]{2,1,0:T(8,128)S(1)}, u32[]{:S(2)}, u32[]{:S(2)}) collective-permute-start(f32[33,8,128]{2,1,0:T(8,128)S(1)} %back1_other.7), channel_id=1, source_target_pairs={{0,16},{8,24},{16,0},{24,8},{32,48},{40,56},{48,32},{56,40},{64,80... | collective-permute-start | bytes 405512 | tf_op jit(solution)/shard_map/ppermute | solution.py:207
  165.8 6.7 %collective-permute-start.19 = (f32[33,8,128]{2,1,0:T(8,128)S(1)}, f32[33,8,128]{2,1,0:T(8,128)S(1)}, u32[]{:S(2)}, u32[]{:S(2)}) collective-permute-start(f32[33,8,128]{2,1,0:T(8,128)S(1)} %get-tuple-element.42.send_ref), channel_id=1, source_target_pairs={{0,1},{1,0},{2,3},{3,2},{4,5},{5,4},{6,7},{7,6},{8,9},{9,8},{10,11... | collective-permute-start | bytes 405512 | tf_op jit(solution)/shard_map/ppermute | solution.py:269
  171.5 26.2 %copy-start = (f32[1024,64]{0,1:T(8,128)S(1)}, f32[1024,64]{0,1:T(8,128)}, u32[]{:S(2)}) copy-start(f32[1024,64]{0,1:T(8,128)} %param.4) | copy-start | bytes 786436
  171.5 26.2 %copy-start.1 = (f32[64]{0:T(128)S(1)}, f32[64]{0:T(128)}, u32[]{:S(2)}) copy-start(f32[64]{0:T(128)} %param.5) | copy-start | bytes 772
  172.5 6.4 %collective-permute-start.22 = (f32[33,8,128]{2,1,0:T(8,128)S(1)}, f32[33,8,128]{2,1,0:T(8,128)S(1)}, u32[]{:S(2)}, u32[]{:S(2)}) collective-permute-start(f32[33,8,128]{2,1,0:T(8,128)S(1)} %add.5.refs_0_), channel_id=1, source_target_pairs={{0,4},{1,5},{2,6},{3,7},{4,0},{5,1},{6,2},{7,3},{8,12},{9,13},{10,... | collective-permute-start | bytes 405512 | tf_op jit(solution)/shard_map/ppermute | solution.py:272
  174.1 8.3 %collective-permute-start.21 = (f32[33,8,128]{2,1,0:T(8,128)S(1)}, f32[33,8,128]{2,1,0:T(8,128)S(1)}, u32[]{:S(2)}, u32[]{:S(2)}) collective-permute-start(f32[33,8,128]{2,1,0:T(8,128)S(1)} %add.5.refs_0_), channel_id=1, source_target_pairs={{0,2},{1,3},{2,4},{3,5},{4,6},{5,7},{6,0},{7,1},{8,10},{9,11},{10,... | collective-permute-start | bytes 405512 | tf_op jit(solution)/shard_map/ppermute | solution.py:272
  175.5 6.9 %collective-permute-start.20 = (f32[33,8,128]{2,1,0:T(8,128)S(1)}, f32[33,8,128]{2,1,0:T(8,128)S(1)}, u32[]{:S(2)}, u32[]{:S(2)}) collective-permute-start(f32[33,8,128]{2,1,0:T(8,128)S(1)} %add.5.refs_0_), channel_id=1, source_target_pairs={{0,6},{1,7},{2,0},{3,1},{4,2},{5,3},{6,4},{7,5},{8,14},{9,15},{10,... | collective-permute-start | bytes 405512 | tf_op jit(solution)/shard_map/ppermute | solution.py:272
  182.5 1.6 collective-permute-start.23

commit v2 on v1

--- a/solution.py
+++ b/solution.py
@@ -11,6 +11,7 @@
 Y_SHIFTS = [[(i, (i + NC * k) % (NY * NC)) for i in range(NY * NC)] for k in (3, 1, 2)]
 X_SHIFTS = [[(i, i // NX * NX + (i + k) % NX) for i in range(NZ * NX)] for k in range(NX)]
 GROUPS_Z = [[z * NX + x for z in range(NZ)] for x in range(NX)]
+SENT = (2, 1, 3)
 CORE_SWAP = [(i, i ^ 1) for i in range(NY * NC)]
 
 T = 64
@@ -249,11 +250,19 @@
 ):
     e0, e1 = basis01(g_ref, own0_ref, w1_ref, own1_ref)
     overlap0, overlap1 = columns_of(tile_ref[...], 2)
-    q = wide(w_ref) - overlap0 * e0 - overlap1 * e1
+    q = (wide(w_ref) - overlap0 * e0 - overlap1 * e1) * (1.0 / jnp.maximum(overlap1, TINY))
     q_ref[...] = q
+    forward_send(q, [jnp.zeros((1, T), f32)], high_ref, low_ref, send_ref, both_ref)
+
+
+def keep2_kernel(both_ref, g_ref, own0_ref, w1_ref, own1_ref, q_ref, high_ref, low_ref, keep_ref):
+    both = both_ref[...]
+    at = half_rows(True)
+    put_half(keep_ref, product(both, both[:T], high_ref[:, at], low_ref[:, at]))
+    e0, e1 = basis01(g_ref, own0_ref, w1_ref, own1_ref)
+    q = q_ref[...]
     pairs = [(e0, e0), (e0, e1), (e0, q), (e1, e1), (e1, q), (q, q)]
-    scalars = [row_of(p * q) for p, q in pairs]
-    forward_send(q, scalars, high_ref, low_ref, send_ref, both_ref)
+    keep_ref[TILES] = rows_tile([row_of(left * right) for left, right in pairs])
 
 
 def keep_kernel(both_ref, send_ref, high_ref, low_ref, keep_ref):
@@ -263,15 +272,19 @@
     keep_ref[TILES] = send_ref[TILES]
 
 
-def sum_over_feat(kernel, args, turned, name, extra=()):
-    outs = [HALF, ((2 * T, F), bf16), *extra]
-    send, both, *extra = call(kernel, outs, name)(*args, *turned)
+def sum_over_feat(kernel, args, turned, name):
+    outs = [HALF, ((2 * T, F), bf16)]
+    send, both = call(kernel, outs, name)(*args, *turned)
     got = lax.ppermute(send, "feat", CORE_SWAP)
     (keep,) = call(keep_kernel, [HALF], "keep")(both, send, *turned)
+    return add_over_feat(keep, got)
+
+
+def add_over_feat(keep, got):
     (part,) = call(add_kernel, [HALF], "add")(keep, got)
     got = [lax.ppermute(part, "feat", shift) for shift in Y_SHIFTS]
     (own,) = call(add_kernel, [HALF], "sum_y")(part, *got)
-    return own, lax.ppermute(own, "feat", CORE_SWAP), *extra
+    return own, lax.ppermute(own, "feat", CORE_SWAP)
 
 
 def image0(tile_ref, half0_ref):
@@ -292,27 +305,34 @@
         out_ref[x] = product(both, high, high_ref[rows, at], low_ref[rows, at])
 
 
-def ready(value, both_ref):
-    high, low = split(value)
-    both_ref[...] = jnp.concatenate([high, low], axis=0)
-
-
-def back_other_kernel(shift, both_ref, acc_ref, high_ref, low_ref, *refs):
-    both = both_ref[...]
+def back_quarter(shift, both, acc_ref, high_ref, low_ref, out_ref, *tiles):
     rows = half_rows(False)
     place, at = quarter(shift)
-    out_ref = refs[-1]
     put_half(out_ref, acc_ref[place] + product(both, both[:T], high_ref[rows, at], low_ref[rows, at]))
-    for tile_ref in refs[:-1]:
-        out_ref[NZ * LINE] = tile_ref[...]
+    for tile in tiles:
+        out_ref[NZ * LINE] = tile
+
+
+def back_others(value, acc_ref, high_ref, low_ref, out_refs, both_ref, *tiles):
+    high, low = split(value)
+    both = jnp.concatenate([high, low], axis=0)
+    both_ref[...] = both
+    for shift, out_ref in zip(SENT, out_refs):
+        back_quarter(shift, both, acc_ref, high_ref, low_ref, out_ref, *tiles)
+
+
+def back_mine_kernel(both_ref, acc_ref, high_ref, low_ref, *refs):
+    tiles = [ref[...] for ref in refs[:-1]]
+    back_quarter(0, both_ref[...], acc_ref, high_ref, low_ref, refs[-1], *tiles)
 
 
 def back0_own_kernel(own0_ref, high_ref, low_ref, out_ref):
     back_own(image0(own0_ref, own0_ref), high_ref, low_ref, out_ref)
 
 
-def back0_ready_kernel(own0_ref, other0_ref, both_ref):
-    ready(image0(own0_ref, other0_ref), both_ref)
+def back0_others_kernel(own0_ref, other0_ref, acc_ref, high_ref, low_ref, *refs):
+    value = image0(own0_ref, other0_ref)
+    back_others(value, acc_ref, high_ref, low_ref, refs[:-1], refs[-1])
 
 
 def overlaps(u0, u1):
@@ -325,59 +345,52 @@
     tile_ref[...] = overlaps(image0(own0_ref, own0_ref), u1)
 
 
-def back1_ready_kernel(own0_ref, other0_ref, own1_ref, other1_ref, tile_ref, both_ref, out_tile_ref):
-    u1 = image1(own0_ref, other0_ref, own1_ref, other1_ref)
-    ready(u1, both_ref)
-    out_tile_ref[...] = tile_ref[...] + overlaps(image0(own0_ref, other0_ref), u1)
-
-
-def transposed(own_kernel, ready_kernel, owns, halves, a_high, a_low, tiles, name):
+def back1_others_kernel(
+    own0_ref, other0_ref, own1_ref, other1_ref, tile_ref, acc_ref, high_ref, low_ref, *refs
+):
+    value = image1(own0_ref, other0_ref, own1_ref, other1_ref)
+    tile = tile_ref[...] + overlaps(image0(own0_ref, other0_ref), value)
+    refs[-1][...] = tile
+    back_others(value, acc_ref, high_ref, low_ref, refs[:-2], refs[-2], tile)
+
+
+def transposed(own_kernel, others_kernel, owns, halves, a_high, a_low, tiles, name):
     tile = [((8, 128), f32)] * tiles
     outs = [((NX, T, FB), f32)] + tile
     acc, *scalars = call(own_kernel, outs, name + "_own")(*owns, a_high, a_low)
-    outs = [((2 * T, H), bf16)] + tile
-    both, *scalars = call(ready_kernel, outs, name + "_ready")(*halves, *scalars)
-    parts = [None] * NX
     (count, *rest), dtype = QUARTER
-    for k in (2, 1, 3, 0):
-        kernel = functools.partial(back_other_kernel, k)
-        outs = [((count + tiles, *rest), dtype)]
-        (parts[k],) = call(kernel, outs, name + "_other")(both, acc, a_high, a_low, *scalars)
-    return parts
+    part = ((count + tiles, *rest), dtype)
+    outs = [part] * len(SENT) + [((2 * T, H), bf16)] + tile
+    args = (*halves, *scalars, acc, a_high, a_low)
+    results = call(others_kernel, outs, name + "_others")(*args)
+    sent, (both, *scalars) = results[: len(SENT)], results[len(SENT) :]
+    (mine,) = call(back_mine_kernel, [part], name + "_mine")(both, acc, a_high, a_low, *scalars)
+    return {0: mine, **dict(zip(SENT, sent))}
 
 
 PAIRS = [(0, 0), (0, 1), (0, 2), (1, 1), (1, 2), (2, 2)]
 
 
-def images(own0_ref, own1_ref, own2_ref, half0_ref, half1_ref, half2_ref):
-    u0 = image0(own0_ref, half0_ref)
-    u1 = image1(own0_ref, half0_ref, own1_ref, half1_ref)
-    square = columns_of(tile_in(own2_ref), 6)[5]
-    return u0, u1, half_in(half2_ref) * lax.rsqrt(jnp.maximum(square, TINY))
-
-
-def gram_rows(*refs):
-    u = images(*refs)
+def gram_rows(own, u_ref, half2_ref):
+    at = half_rows(own)
+    u = u_ref[0, :, at], u_ref[1, :, at], half_in(half2_ref)
     return rows_tile([row_of(u[i] * u[j]) for i, j in PAIRS])
 
 
-def gram_own_kernel(own0_ref, own1_ref, own2_ref, out_ref):
-    out_ref[...] = gram_rows(own0_ref, own1_ref, own2_ref, own0_ref, own1_ref, own2_ref)
-
-
-def gram_kernel(own0_ref, other0_ref, own1_ref, other1_ref, own2_ref, other2_ref, tile_ref, out_ref):
-    tile = tile_ref[...]
-    tile += gram_rows(own0_ref, own1_ref, own2_ref, other0_ref, other1_ref, other2_ref)
+def gram_own_kernel(u_ref, own2_ref, out_ref):
+    out_ref[...] = gram_rows(True, u_ref, own2_ref)
+
+
+def gram_kernel(u_ref, other2_ref, tile_ref, out_ref):
+    tile = tile_ref[...] + gram_rows(False, u_ref, other2_ref)
     for i in range(out_ref.shape[0]):
         out_ref[i] = tile
 
 
 def solve(gram, dots, square0, ridge):
-    scale2 = lax.rsqrt(jnp.maximum(dots[5], TINY))
-    e = [dots[0], dots[1], dots[2] * scale2, dots[3], dots[4] * scale2, dots[5] * scale2 * scale2]
-    k00, k01, k02, k11, k12, k22 = [u + ridge * v for u, v in zip(gram, e)]
+    k00, k01, k02, k11, k12, k22 = [u + ridge * v for u, v in zip(gram, dots)]
     norm = jnp.sqrt(square0)
-    r0, r1, r2 = e[0] * norm, e[1] * norm, e[2] * norm
+    r0, r1, r2 = dots[0] * norm, dots[1] * norm, dots[2] * norm
     inverse0 = 1.0 / jnp.maximum(k00, TINY)
     l10, l20 = k01 * inverse0, k02 * inverse0
     d1 = k11 - l10 * k01
@@ -391,17 +404,24 @@
     c2 = z2 * inverse2
     c1 = z1 * inverse1 - l21 * c2
     c0 = r0 * inverse0 - l10 * c1 - l20 * c2
-    return c0, c1, c2, c2 * scale2
+    return c0, c1, c2
+
+
+def basis_kernel(g_ref, own0_ref, w1_ref, own1_ref, other0_ref, other1_ref, e_ref, u_ref):
+    e_ref[0], e_ref[1] = basis01(g_ref, own0_ref, w1_ref, own1_ref)
+    for own, half0_ref, half1_ref in ((True, own0_ref, own1_ref), (False, other0_ref, other1_ref)):
+        at = half_rows(own)
+        u_ref[0, :, at] = image0(own0_ref, half0_ref)
+        u_ref[1, :, at] = image1(own0_ref, half0_ref, own1_ref, half1_ref)
 
 
 def last_kernel(
-    gram_ref, ridge_ref, b_ref, g_ref, w1_ref, q_ref,
-    own0_ref, other0_ref, own1_ref, other1_ref, own2_ref, other2_ref, x_ref, r_ref,
+    gram_ref, ridge_ref, b_ref, e_ref, q_ref, u_ref, own0_ref, own2_ref, other2_ref, x_ref, r_ref
 ):
     gram = gram_ref[0]
     for i in range(1, gram_ref.shape[0]):
         gram = gram + gram_ref[i]
-    dots = tile_in(own2_ref)
+    dots = tile_in(own2_ref) + tile_in(other2_ref)
     row = lambda tile, i: tile[i : i + 1, :]
     coefficients = solve(
         [row(gram, i) for i in range(6)],
@@ -409,18 +429,12 @@
         row(tile_in(own0_ref), 0),
         jnp.concatenate([ridge_ref[...], jnp.zeros((1, 128 - T), f32)], axis=1),
     )
-    tile = jnp.concatenate(list(coefficients) + [jnp.zeros((4, 128), f32)], axis=0)
-    c0, c1, _, c2 = columns_of(tile, 4)
-    e0, e1 = basis01(g_ref, own0_ref, w1_ref, own1_ref)
-    x_ref[...] = c0 * e0 + c1 * e1 + c2 * q_ref[...]
-    for own, half0_ref, half1_ref, half2_ref in (
-        (True, own0_ref, own1_ref, own2_ref),
-        (False, other0_ref, other1_ref, other2_ref),
-    ):
-        u0 = image0(own0_ref, half0_ref)
-        u1 = image1(own0_ref, half0_ref, own1_ref, half1_ref)
+    tile = jnp.concatenate(list(coefficients) + [jnp.zeros((5, 128), f32)], axis=0)
+    c0, c1, c2 = columns_of(tile, 3)
+    x_ref[...] = c0 * e_ref[0] + c1 * e_ref[1] + c2 * q_ref[...]
+    for own, half2_ref in ((True, own2_ref), (False, other2_ref)):
         at = half_rows(own)
-        r_ref[:, at] = b_ref[:, at] - c0 * u0 - c1 * u1 - c2 * half_in(half2_ref)
+        r_ref[:, at] = b_ref[:, at] - c0 * u_ref[0, :, at] - c1 * u_ref[1, :, at] - c2 * half_in(half2_ref)
 
 
 def last(*args):
@@ -446,22 +460,27 @@
     (g,) = sum_over_samp(parts)
     own0, other0 = sum_over_feat(send0_kernel, (g,), turned, "send0")
     parts = transposed(
-        back0_own_kernel, back0_ready_kernel, (own0,), (own0, other0), a_high, a_low, 0, "back0"
+        back0_own_kernel, back0_others_kernel, (own0,), (own0, other0), a_high, a_low, 0, "back0"
     )
     (w1,) = sum_over_samp(parts)
     own1, other1 = sum_over_feat(send1_kernel, (g, own0, w1), turned, "send1")
     halves = (own0, other0, own1, other1)
     parts = transposed(
-        back1_own_kernel, back1_ready_kernel, (own0, own1), halves, a_high, a_low, 1, "back1"
+        back1_own_kernel, back1_others_kernel, (own0, own1), halves, a_high, a_low, 1, "back1"
     )
     w2, tile = sum_over_samp(parts)
-    args = (g, own0, w1, own1, w2, tile)
-    own2, other2, q = sum_over_feat(send2_kernel, args, turned, "send2", [((T, F), f32)])
-    halves = (own0, other0, own1, other1, own2, other2)
-    (tile,) = call(gram_own_kernel, [((8, 128), f32)], "gram_own")(own0, own1, own2)
-    (tiles,) = call(gram_kernel, [((N, 8, 128), f32)], "gram")(*halves, tile)
+    basis = (g, own0, w1, own1)
+    outs = [HALF, ((2 * T, F), bf16), ((T, F), f32)]
+    send, both, q = call(send2_kernel, outs, "send2")(*basis, w2, tile, *turned)
+    got = lax.ppermute(send, "feat", CORE_SWAP)
+    (keep,) = call(keep2_kernel, [HALF], "keep2")(both, *basis, q, *turned)
+    own2, other2 = add_over_feat(keep, got)
+    outs = [((2, T, F), f32), ((2, T, S), f32)]
+    e, u = call(basis_kernel, outs, "basis")(*basis, other0, other1)
+    (tile,) = call(gram_own_kernel, [((8, 128), f32)], "gram_own")(u, own2)
+    (tiles,) = call(gram_kernel, [((N, 8, 128), f32)], "gram")(u, other2, tile)
     gram = lax.all_to_all(tiles, "samp", 0, 0)
-    x, r = last(gram, ridge.reshape(1, T), b_t, g, w1, q, *halves)
+    x, r = last(gram, ridge.reshape(1, T), b_t, e, q, u, own0, own2, other2)
     return x.T, r.T
 
 

time: 200 us -> 198 us (0.990)
    ppermute x3 -> x2, starting transfers between devices: 17.6 us -> 11.9 us  [sum_over_feat(): got = lax.ppermute(send, 'feat', CORE_SWAP)]
    ppermute x12 -> x13, starting transfers between devices: 17.4 us -> 23.1 us  [the longest x9 14.5 us: add_over_feat(): got = [lax.ppermute(part, 'feat', shift) for shift in Y_SHIFTS]]
    pallas_call x35 -> x30, Pallas kernels: 15.2 us -> 14.4 us  [run(): pl.pallas_call(kernel, in_specs=[VMEM] * len(args), out_specs=[VMEM] * le...]
    ppermute x12 -> x13, waiting for transfers between devices: 15.6 us -> 15.3 us  [the longest x9 15.1 us: add_over_feat(): got = [lax.ppermute(part, 'feat', shift) for shift in Y_SHIFTS]]
  transfers between devices with their start and end apart: 24 -> 24, of which waited for: 17 -> 16; matrix products, arithmetic and copies ran while one was open for 0% -> 0% of each run, Pallas kernels for 4% -> 4%
where the time goes in v2:
time: 198 us
  blocking collectives  99.9 us (50%)
  starting transfers between devices  46.7 us (24%)
  waiting for transfers between devices  30.1 us (15%)
  Pallas kernels  20.3 us (10%)
    all_to_all x3, blocking collectives, sum_over_samp(): return (lax.all_to_all(part, 'samp', 0, 0), *tile)  49.4 us
    all_to_all x3, blocking collectives, sum_over_samp(): got = lax.all_to_all(part, 'samp', 0, 0, axis_index_groups=GROUPS_Z)  37.4 us
    ppermute x9, waiting for transfers between devices, add_over_feat(): got = [lax.ppermute(part, 'feat', shift) for shift in Y_SHIFTS]  15.1 us
    ppermute x9, starting transfers between devices, add_over_feat(): got = [lax.ppermute(part, 'feat', shift) for shift in Y_SHIFTS]  14.5 us
    pallas_call x30, Pallas kernels, run(): pl.pallas_call(kernel, in_specs=[VMEM] * len(args), out_specs=[VMEM] * le...  14.4 us
    ppermute x9, waiting for transfers between devices, sum_over_samp(): got = [lax.ppermute(parts[k], 'samp', X_SHIFTS[k]) for k in (3, 1, 2)]  14.4 us
    all_to_all x1, blocking collectives, per_device(): gram = lax.all_to_all(tiles, 'samp', 0, 0)  13.1 us
    ppermute x2, starting transfers between devices, sum_over_feat(): got = lax.ppermute(send, 'feat', CORE_SWAP)  11.9 us
  transfers between devices with their start and end apart: 24, of which 16 were waited for; matrix products, arithmetic and copies ran while one was open for 0% of the time, Pallas kernels for 4%

profile of v2, /device:TPU:1, one launch (start us, length us, event | category | flops | bytes accessed | tf_op | source)
XLA Modules:
  0.0 197.9 jit_solution(916251847868155754)
XLA Ops:
  0.6 4.6 %first.1 = (f32[32,8,128]{2,1,0:T(8,128)S(1)}, bf16[128,1024]{1,0:T(8,128)(2,1)S(1)}, bf16[1024,2048]{1,0:T(8,128)(2,1)S(1)}, bf16[1024,2048]{1,0:T(8,128)(2,1)S(1)}) custom-call(f32[1024,2048]{1,0:T(8,128)} %a_hbm.1, f32[64,1024]{1,0:T(8,128)} %bitcast.4), custom_call_target="tpu_custom_call" | custom-call | tf_op jit(solution)/shard_map/first/pallas_call | solution.py:157
  5.7 3.4 %collective-permute-start = (f32[32,8,128]{2,1,0:T(8,128)S(1)}, f32[32,8,128]{2,1,0:T(8,128)S(1)}, u32[]{:S(2)}, u32[]{:S(2)}) collective-permute-start(f32[32,8,128]{2,1,0:T(8,128)S(1)} %first_more.2), channel_id=1, source_target_pairs={{0,24},{8,0},{16,8},{24,16},{32,56},{40,32},{48,40},{56,48},{64,88... | collective-permute-start | bytes 393224 | tf_op jit(solution)/shard_map/ppermute | solution.py:208
  9.7 1.7 collective-permute-start.2
  11.3 2.5 %first_last.1 = (f32[32,8,128]{2,1,0:T(8,128)S(1)}, bf16[2048,1024]{1,0:T(8,128)(2,1)S(1)}, bf16[2048,1024]{1,0:T(8,128)(2,1)S(1)}) custom-call(bf16[128,1024]{1,0:T(8,128)(2,1)S(1)} %get-tuple-element.33.both_ref, bf16[1024,2048]{1,0:T(8,128)(2,1)S(1)} %get-tuple-element.34.high_ref, bf16[1024,2048]{1,0:T(8,128)(2,1)S(1)} %get-tuple-element.35.low_ref), custom_call_target="tpu_custom_call" | custom-call | tf_op jit(solution)/shard_map/first_last/pallas_call | solution.py:39
  13.8 3.2 %collective-permute-done.1.refs_2_ = f32[32,8,128]{2,1,0:T(8,128)S(1)} collective-permute-done((f32[32,8,128]{2,1,0:T(8,128)S(1)}, f32[32,8,128]{2,1,0:T(8,128)S(1)}, u32[]{:S(2)}, u32[]{:S(2)}) %collective-permute-start.1) | collective-permute-done | bytes 131104 | tf_op jit(solution)/shard_map/ppermute | solution.py:208
  17.1 15.8 %all_to_all.35.in_ref = f32[8,4,8,128]{3,2,1,0:T(8,128)S(1)} all-to-all(f32[8,4,8,128]{3,2,1,0:T(8,128)S(1)} %sum_x.3), channel_id=1, replica_groups={{0,32,64,96,128,160,192,224},{8,40,72,104,136,168,200,232},{16,48,80,11..., dimensions={0} | all-to-all | bytes 262144 | tf_op jit(solution)/shard_map/all_to_all | solution.py:210
  32.9 16.1 %all_to_all.36.g_ref = f32[32,8,512]{2,1,0:T(8,128)S(1)} all-to-all(f32[32,8,512]{2,1,0:T(8,128)S(1)} %sum_z.3), channel_id=1, replica_groups=mesh['samp'=32,'feat'=8] {'samp'}, dimensions={0} | all-to-all | bytes 1048576 | tf_op jit(solution)/shard_map/all_to_all | solution.py:213
  49.8 6.2 %collective-permute-start.3 = (f32[33,8,128]{2,1,0:T(8,128)S(1)}, f32[33,8,128]{2,1,0:T(8,128)S(1)}, u32[]{:S(2)}, u32[]{:S(2)}) collective-permute-start(f32[33,8,128]{2,1,0:T(8,128)S(1)} %get-tuple-element.41.send_ref), channel_id=1, source_target_pairs={{0,1},{1,0},{2,3},{3,2},{4,5},{5,4},{6,7},{7,6},{8,9},{9,8},{10,11... | collective-permute-start | bytes 405512 | tf_op jit(solution)/shard_map/ppermute | solution.py:278
  57.1 3.0 %collective-permute-start.6 = (f32[33,8,128]{2,1,0:T(8,128)S(1)}, f32[33,8,128]{2,1,0:T(8,128)S(1)}, u32[]{:S(2)}, u32[]{:S(2)}) collective-permute-start(f32[33,8,128]{2,1,0:T(8,128)S(1)} %add.3.refs_0_), channel_id=1, source_target_pairs={{0,4},{1,5},{2,6},{3,7},{4,0},{5,1},{6,2},{7,3},{8,12},{9,13},{10,... | collective-permute-start | bytes 405512 | tf_op jit(solution)/shard_map/ppermute | solution.py:285
  60.5 2.3 %collective-permute-start.4 = (f32[33,8,128]{2,1,0:T(8,128)S(1)}, f32[33,8,128]{2,1,0:T(8,128)S(1)}, u32[]{:S(2)}, u32[]{:S(2)}) collective-permute-start(f32[33,8,128]{2,1,0:T(8,128)S(1)} %add.3.refs_0_), channel_id=1, source_target_pairs={{0,6},{1,7},{2,0},{3,1},{4,2},{5,3},{6,4},{7,5},{8,14},{9,15},{10,... | collective-permute-start | bytes 405512 | tf_op jit(solution)/shard_map/ppermute | solution.py:285
  63.5 3.4 %collective-permute-done.5.refs_2_ = f32[33,8,128]{2,1,0:T(8,128)S(1)} collective-permute-done((f32[33,8,128]{2,1,0:T(8,128)S(1)}, f32[33,8,128]{2,1,0:T(8,128)S(1)}, u32[]{:S(2)}, u32[]{:S(2)}) %collective-permute-start.5) | collective-permute-done | bytes 135200 | tf_op jit(solution)/shard_map/ppermute | solution.py:285
  70.0 1.6 collective-permute-start.8
  71.6 1.7 collective-permute-start.10
  74.8 3.7 %collective-permute-done.9.refs_2_ = f32[32,8,128]{2,1,0:T(8,128)S(1)} collective-permute-done((f32[32,8,128]{2,1,0:T(8,128)S(1)}, f32[32,8,128]{2,1,0:T(8,128)S(1)}, u32[]{:S(2)}, u32[]{:S(2)}) %collective-permute-start.9) | collective-permute-done | bytes 131104 | tf_op jit(solution)/shard_map/ppermute | solution.py:208
  79.1 10.7 %all_to_all.37.in_ref = f32[8,4,8,128]{3,2,1,0:T(8,128)S(1)} all-to-all(f32[8,4,8,128]{3,2,1,0:T(8,128)S(1)} %sum_x.4), channel_id=1, replica_groups={{0,32,64,96,128,160,192,224},{8,40,72,104,136,168,200,232},{16,48,80,11..., dimensions={0} | all-to-all | bytes 262144 | tf_op jit(solution)/shard_map/all_to_all | solution.py:210
  89.9 16.6 %all_to_all.38.w_ref.w1_ref = f32[32,8,512]{2,1,0:T(8,128)S(1)} all-to-all(f32[32,8,512]{2,1,0:T(8,128)S(1)} %sum_z.4), channel_id=1, replica_groups=mesh['samp'=32,'feat'=8] {'samp'}, dimensions={0} | all-to-all | bytes 1048576 | tf_op jit(solution)/shard_map/all_to_all | solution.py:213
  107.3 5.6 %collective-permute-start.11 = (f32[33,8,128]{2,1,0:T(8,128)S(1)}, f32[33,8,128]{2,1,0:T(8,128)S(1)}, u32[]{:S(2)}, u32[]{:S(2)}) collective-permute-start(f32[33,8,128]{2,1,0:T(8,128)S(1)} %get-tuple-element.47.send_ref), channel_id=1, source_target_pairs={{0,1},{1,0},{2,3},{3,2},{4,5},{5,4},{6,7},{7,6},{8,9},{9,8},{10,11... | collective-permute-start | bytes 405512 | tf_op jit(solution)/shard_map/ppermute | solution.py:278
  113.9 1.9 collective-permute-start.14
  115.8 1.4 collective-permute-start.13
  118.5 1.9 collective-permute-done.14.refs_3_
  120.3 3.4 %collective-permute-done.13.refs_2_ = f32[33,8,128]{2,1,0:T(8,128)S(1)} collective-permute-done((f32[33,8,128]{2,1,0:T(8,128)S(1)}, f32[33,8,128]{2,1,0:T(8,128)S(1)}, u32[]{:S(2)}, u32[]{:S(2)}) %collective-permute-start.13) | collective-permute-done | bytes 135200 | tf_op jit(solution)/shard_map/ppermute | solution.py:285
  126.8 1.5 collective-permute-start.16
  128.3 1.7 collective-permute-start.18
  130.3 1.5 collective-permute-done.16.refs_1_
  131.8 3.3 %collective-permute-done.17.refs_2_ = f32[33,8,128]{2,1,0:T(8,128)S(1)} collective-permute-done((f32[33,8,128]{2,1,0:T(8,128)S(1)}, f32[33,8,128]{2,1,0:T(8,128)S(1)}, u32[]{:S(2)}, u32[]{:S(2)}) %collective-permute-start.17) | collective-permute-done | bytes 135200 | tf_op jit(solution)/shard_map/ppermute | solution.py:208
  136.1 10.9 %all_to_all.39.in_ref = f32[8,5,8,128]{3,2,1,0:T(8,128)S(1)} all-to-all(f32[8,5,8,128]{3,2,1,0:T(8,128)S(1)} %sum_x.5), channel_id=1, replica_groups={{0,32,64,96,128,160,192,224},{8,40,72,104,136,168,200,232},{16,48,80,11..., dimensions={0} | all-to-all | bytes 327680 | tf_op jit(solution)/shard_map/all_to_all | solution.py:210
  147.0 16.8 %all_to_all.40.w_ref = f32[32,8,512]{2,1,0:T(8,128)S(1)} all-to-all(f32[32,8,512]{2,1,0:T(8,128)S(1)} %get-tuple-element.56), channel_id=1, replica_groups=mesh['samp'=32,'feat'=8] {'samp'}, dimensions={0} | all-to-all | bytes 1048576 | tf_op jit(solution)/shard_map/all_to_all | solution.py:213
  164.9 5.7 %collective-permute-start.19 = (f32[33,8,128]{2,1,0:T(8,128)S(1)}, f32[33,8,128]{2,1,0:T(8,128)S(1)}, u32[]{:S(2)}, u32[]{:S(2)}) collective-permute-start(f32[33,8,128]{2,1,0:T(8,128)S(1)} %get-tuple-element.60), channel_id=1, source_target_pairs={{0,1},{1,0},{2,3},{3,2},{4,5},{5,4},{6,7},{7,6},{8,9},{9,8},{10,11... | collective-permute-start | bytes 405512 | tf_op jit(solution)/shard_map/ppermute | solution.py:475
  171.7 1.7 collective-permute-start.22
  176.0 2.2 %collective-permute-done.22.refs_3_ = f32[33,8,128]{2,1,0:T(8,128)S(1)} collective-permute-done((f32[33,8,128]{2,1,0:T(8,128)S(1)}, f32[33,8,128]{2,1,0:T(8,128)S(1)}, u32[]{:S(2)}, u32[]{:S(2)}) %collective-permute-start.22) | collective-permute-done | bytes 135200 | tf_op jit(solution)/shard_map/ppermute | solution.py:285
  178.2 3.5 %collective-permute-done.21.refs_2_ = f32[33,8,128]{2,1,0:T(8,128)S(1)} collective-permute-done((f32[33,8,128]{2,1,0:T(8,128)S(1)}, f32[33,8,128]{2,1,0:T(8,128)S(1)}, u32[]{:S(2)}, u32[]{:S(2)}) %collective-permute-start.21) | collective-permute-done | bytes 135200 | tf_op jit(solution)/shard_map/ppermute | solution.py:285
  183.5 13.1 %all_to_all.41.gram_ref = f32[32,8,128]{2,1,0:T(8,128)S(1)} all-to-all(f32[32,8,128]{2,1,0:T(8,128)S(1)} %gram.1), channel_id=1, replica_groups=mesh['samp'=32,'feat'=8] {'samp'}, dimensions={0} | all-to-all | bytes 262144 | tf_op jit(solution)/shard_map/all_to_all | solution.py:482
  (59 shorter events, 24.7 us)
Async XLA Ops:
  5.7 8.1 %collective-permute-start = (f32[32,8,128]{2,1,0:T(8,128)S(1)}, f32[32,8,128]{2,1,0:T(8,128)S(1)}, u32[]{:S(2)}, u32[]{:S(2)}) collective-permute-start(f32[32,8,128]{2,1,0:T(8,128)S(1)} %first_more.2), channel_id=1, source_target_pairs={{0,24},{8,0},{16,8},{24,16},{32,56},{40,32},{48,40},{56,48},{64,88... | collective-permute-start | bytes 393224 | tf_op jit(solution)/shard_map/ppermute | solution.py:208
  9.6 7.5 %collective-permute-start.1 = (f32[32,8,128]{2,1,0:T(8,128)S(1)}, f32[32,8,128]{2,1,0:T(8,128)S(1)}, u32[]{:S(2)}, u32[]{:S(2)}) collective-permute-start(f32[32,8,128]{2,1,0:T(8,128)S(1)} %first_more.3), channel_id=1, source_target_pairs={{0,8},{8,16},{16,24},{24,0},{32,40},{40,48},{48,56},{56,32},{64,72... | collective-permute-start | bytes 393224 | tf_op jit(solution)/shard_map/ppermute | solution.py:208
  9.7 7.4 %collective-permute-start.2 = (f32[32,8,128]{2,1,0:T(8,128)S(1)}, f32[32,8,128]{2,1,0:T(8,128)S(1)}, u32[]{:S(2)}, u32[]{:S(2)}) collective-permute-start(f32[32,8,128]{2,1,0:T(8,128)S(1)} %get-tuple-element.37), channel_id=1, source_target_pairs={{0,16},{8,24},{16,0},{24,8},{32,48},{40,56},{48,32},{56,40},{64,80... | collective-permute-start | bytes 393224 | tf_op jit(solution)/shard_map/ppermute | solution.py:208
  49.8 7.2 %collective-permute-start.3 = (f32[33,8,128]{2,1,0:T(8,128)S(1)}, f32[33,8,128]{2,1,0:T(8,128)S(1)}, u32[]{:S(2)}, u32[]{:S(2)}) collective-permute-start(f32[33,8,128]{2,1,0:T(8,128)S(1)} %get-tuple-element.41.send_ref), channel_id=1, source_target_pairs={{0,1},{1,0},{2,3},{3,2},{4,5},{5,4},{6,7},{7,6},{8,9},{9,8},{10,11... | collective-permute-start | bytes 405512 | tf_op jit(solution)/shard_map/ppermute | solution.py:278
  57.1 6.4 %collective-permute-start.6 = (f32[33,8,128]{2,1,0:T(8,128)S(1)}, f32[33,8,128]{2,1,0:T(8,128)S(1)}, u32[]{:S(2)}, u32[]{:S(2)}) collective-permute-start(f32[33,8,128]{2,1,0:T(8,128)S(1)} %add.3.refs_0_), channel_id=1, source_target_pairs={{0,4},{1,5},{2,6},{3,7},{4,0},{5,1},{6,2},{7,3},{8,12},{9,13},{10,... | collective-permute-start | bytes 405512 | tf_op jit(solution)/shard_map/ppermute | solution.py:285
  60.1 6.8 %collective-permute-start.5 = (f32[33,8,128]{2,1,0:T(8,128)S(1)}, f32[33,8,128]{2,1,0:T(8,128)S(1)}, u32[]{:S(2)}, u32[]{:S(2)}) collective-permute-start(f32[33,8,128]{2,1,0:T(8,128)S(1)} %add.3.refs_0_), channel_id=1, source_target_pairs={{0,2},{1,3},{2,4},{3,5},{4,6},{5,7},{6,0},{7,1},{8,10},{9,11},{10,... | collective-permute-start | bytes 405512 | tf_op jit(solution)/shard_map/ppermute | solution.py:285
  60.5 6.4 %collective-permute-start.4 = (f32[33,8,128]{2,1,0:T(8,128)S(1)}, f32[33,8,128]{2,1,0:T(8,128)S(1)}, u32[]{:S(2)}, u32[]{:S(2)}) collective-permute-start(f32[33,8,128]{2,1,0:T(8,128)S(1)} %add.3.refs_0_), channel_id=1, source_target_pairs={{0,6},{1,7},{2,0},{3,1},{4,2},{5,3},{6,4},{7,5},{8,14},{9,15},{10,... | collective-permute-start | bytes 405512 | tf_op jit(solution)/shard_map/ppermute | solution.py:285
  66.9 2.3 %collective-permute-start.7 = (f32[33,8,128]{2,1,0:T(8,128)S(1)}, f32[33,8,128]{2,1,0:T(8,128)S(1)}, u32[]{:S(2)}, u32[]{:S(2)}) collective-permute-start(f32[33,8,128]{2,1,0:T(8,128)S(1)} %sum_y.3.own0_ref), channel_id=1, source_target_pairs={{0,1},{1,0},{2,3},{3,2},{4,5},{5,4},{6,7},{7,6},{8,9},{9,8},{10,11... | collective-permute-start | bytes 405512 | tf_op jit(solution)/shard_map/ppermute | solution.py:287
  70.0 4.8 %collective-permute-start.8 = (f32[32,8,128]{2,1,0:T(8,128)S(1)}, f32[32,8,128]{2,1,0:T(8,128)S(1)}, u32[]{:S(2)}, u32[]{:S(2)}) collective-permute-start(f32[32,8,128]{2,1,0:T(8,128)S(1)} %get-tuple-element.43), channel_id=1, source_target_pairs={{0,24},{8,0},{16,8},{24,16},{32,56},{40,32},{48,40},{56,48},{64,88... | collective-permute-start | bytes 393224 | tf_op jit(solution)/shard_map/ppermute | solution.py:208
  71.6 6.9 %collective-permute-start.9 = (f32[32,8,128]{2,1,0:T(8,128)S(1)}, f32[32,8,128]{2,1,0:T(8,128)S(1)}, u32[]{:S(2)}, u32[]{:S(2)}) collective-permute-start(f32[32,8,128]{2,1,0:T(8,128)S(1)} %get-tuple-element.44), channel_id=1, source_target_pairs={{0,8},{8,16},{16,24},{24,0},{32,40},{40,48},{48,56},{56,32},{64,72... | collective-permute-start | bytes 393224 | tf_op jit(solution)/shard_map/ppermute | solution.py:208
  71.6 7.5 %collective-permute-start.10 = (f32[32,8,128]{2,1,0:T(8,128)S(1)}, f32[32,8,128]{2,1,0:T(8,128)S(1)}, u32[]{:S(2)}, u32[]{:S(2)}) collective-permute-start(f32[32,8,128]{2,1,0:T(8,128)S(1)} %get-tuple-element.45), channel_id=1, source_target_pairs={{0,16},{8,24},{16,0},{24,8},{32,48},{40,56},{48,32},{56,40},{64,80... | collective-permute-start | bytes 393224 | tf_op jit(solution)/shard_map/ppermute | solution.py:208
  107.3 6.6 %collective-permute-start.11 = (f32[33,8,128]{2,1,0:T(8,128)S(1)}, f32[33,8,128]{2,1,0:T(8,128)S(1)}, u32[]{:S(2)}, u32[]{:S(2)}) collective-permute-start(f32[33,8,128]{2,1,0:T(8,128)S(1)} %get-tuple-element.47.send_ref), channel_id=1, source_target_pairs={{0,1},{1,0},{2,3},{3,2},{4,5},{5,4},{6,7},{7,6},{8,9},{9,8},{10,11... | collective-permute-start | bytes 405512 | tf_op jit(solution)/shard_map/ppermute | solution.py:278
  113.9 6.4 %collective-permute-start.14 = (f32[33,8,128]{2,1,0:T(8,128)S(1)}, f32[33,8,128]{2,1,0:T(8,128)S(1)}, u32[]{:S(2)}, u32[]{:S(2)}) collective-permute-start(f32[33,8,128]{2,1,0:T(8,128)S(1)} %add.4.refs_0_), channel_id=1, source_target_pairs={{0,4},{1,5},{2,6},{3,7},{4,0},{5,1},{6,2},{7,3},{8,12},{9,13},{10,... | collective-permute-start | bytes 405512 | tf_op jit(solution)/shard_map/ppermute | solution.py:285
  115.8 8.0 %collective-permute-start.13 = (f32[33,8,128]{2,1,0:T(8,128)S(1)}, f32[33,8,128]{2,1,0:T(8,128)S(1)}, u32[]{:S(2)}, u32[]{:S(2)}) collective-permute-start(f32[33,8,128]{2,1,0:T(8,128)S(1)} %add.4.refs_0_), channel_id=1, source_target_pairs={{0,2},{1,3},{2,4},{3,5},{4,6},{5,7},{6,0},{7,1},{8,10},{9,11},{10,... | collective-permute-start | bytes 405512 | tf_op jit(solution)/shard_map/ppermute | solution.py:285
  117.2 6.6 %collective-permute-start.12 = (f32[33,8,128]{2,1,0:T(8,128)S(1)}, f32[33,8,128]{2,1,0:T(8,128)S(1)}, u32[]{:S(2)}, u32[]{:S(2)}) collective-permute-start(f32[33,8,128]{2,1,0:T(8,128)S(1)} %add.4.refs_0_), channel_id=1, source_target_pairs={{0,6},{1,7},{2,0},{3,1},{4,2},{5,3},{6,4},{7,5},{8,14},{9,15},{10,... | collective-permute-start | bytes 405512 | tf_op jit(solution)/shard_map/ppermute | solution.py:285
  123.8 2.0 %collective-permute-start.15 = (f32[33,8,128]{2,1,0:T(8,128)S(1)}, f32[33,8,128]{2,1,0:T(8,128)S(1)}, u32[]{:S(2)}, u32[]{:S(2)}) collective-permute-start(f32[33,8,128]{2,1,0:T(8,128)S(1)} %sum_y.4.own1_ref), channel_id=1, source_target_pairs={{0,1},{1,0},{2,3},{3,2},{4,5},{5,4},{6,7},{7,6},{8,9},{9,8},{10,11... | collective-permute-start | bytes 405512 | tf_op jit(solution)/shard_map/ppermute | solution.py:287
  126.8 5.0 %collective-permute-start.16 = (f32[33,8,128]{2,1,0:T(8,128)S(1)}, f32[33,8,128]{2,1,0:T(8,128)S(1)}, u32[]{:S(2)}, u32[]{:S(2)}) collective-permute-start(f32[33,8,128]{2,1,0:T(8,128)S(1)} %get-tuple-element.53), channel_id=1, source_target_pairs={{0,24},{8,0},{16,8},{24,16},{32,56},{40,32},{48,40},{56,48},{64,88... | collective-permute-start | bytes 405512 | tf_op jit(solution)/shard_map/ppermute | solution.py:208
  128.2 6.8 %collective-permute-start.17 = (f32[33,8,128]{2,1,0:T(8,128)S(1)}, f32[33,8,128]{2,1,0:T(8,128)S(1)}, u32[]{:S(2)}, u32[]{:S(2)}) collective-permute-start(f32[33,8,128]{2,1,0:T(8,128)S(1)} %get-tuple-element.54), channel_id=1, source_target_pairs={{0,8},{8,16},{16,24},{24,0},{32,40},{40,48},{48,56},{56,32},{64,72... | collective-permute-start | bytes 405512 | tf_op jit(solution)/shard_map/ppermute | solution.py:208
  128.3 7.7 %collective-permute-start.18 = (f32[33,8,128]{2,1,0:T(8,128)S(1)}, f32[33,8,128]{2,1,0:T(8,128)S(1)}, u32[]{:S(2)}, u32[]{:S(2)}) collective-permute-start(f32[33,8,128]{2,1,0:T(8,128)S(1)} %get-tuple-element.55), channel_id=1, source_target_pairs={{0,16},{8,24},{16,0},{24,8},{32,48},{40,56},{48,32},{56,40},{64,80... | collective-permute-start | bytes 405512 | tf_op jit(solution)/shard_map/ppermute | solution.py:208
  164.9 6.7 %collective-permute-start.19 = (f32[33,8,128]{2,1,0:T(8,128)S(1)}, f32[33,8,128]{2,1,0:T(8,128)S(1)}, u32[]{:S(2)}, u32[]{:S(2)}) collective-permute-start(f32[33,8,128]{2,1,0:T(8,128)S(1)} %get-tuple-element.60), channel_id=1, source_target_pairs={{0,1},{1,0},{2,3},{3,2},{4,5},{5,4},{6,7},{7,6},{8,9},{9,8},{10,11... | collective-permute-start | bytes 405512 | tf_op jit(solution)/shard_map/ppermute | solution.py:475
  171.6 25.0 %copy-start = (f32[1024,64]{0,1:T(8,128)S(1)}, f32[1024,64]{0,1:T(8,128)}, u32[]{:S(2)}) copy-start(f32[1024,64]{0,1:T(8,128)} %param.4) | copy-start | bytes 786436
  171.7 25.0 %copy-start.1 = (f32[64]{0:T(128)S(1)}, f32[64]{0:T(128)}, u32[]{:S(2)}) copy-start(f32[64]{0:T(128)} %param.5) | copy-start | bytes 772
  171.7 6.5 %collective-permute-start.22 = (f32[33,8,128]{2,1,0:T(8,128)S(1)}, f32[33,8,128]{2,1,0:T(8,128)S(1)}, u32[]{:S(2)}, u32[]{:S(2)}) collective-permute-start(f32[33,8,128]{2,1,0:T(8,128)S(1)} %add.5.refs_0_), channel_id=1, source_target_pairs={{0,4},{1,5},{2,6},{3,7},{4,0},{5,1},{6,2},{7,3},{8,12},{9,13},{10,... | collective-permute-start | bytes 405512 | tf_op jit(solution)/shard_map/ppermute | solution.py:285
  173.4 8.3 %collective-permute-start.21 = (f32[33,8,128]{2,1,0:T(8,128)S(1)}, f32[33,8,128]{2,1,0:T(8,128)S(1)}, u32[]{:S(2)}, u32[]{:S(2)}) collective-permute-start(f32[33,8,128]{2,1,0:T(8,128)S(1)} %add.5.refs_0_), channel_id=1, source_target_pairs={{0,2},{1,3},{2,4},{3,5},{4,6},{5,7},{6,0},{7,1},{8,10},{9,11},{10,... | collective-permute-start | bytes 405512 | tf_op jit(solution)/shard_map/ppermute | solution.py:285
  174.8 6.9 %collective-permute-start.20 = (f32[33,8,128]{2,1,0:T(8,128)S(1)}, f32[33,8,128]{2,1,0:T(8,128)S(1)}, u32[]{:S(2)}, u32[]{:S(2)}) collective-permute-start(f32[33,8,128]{2,1,0:T(8,128)S(1)} %add.5.refs_0_), channel_id=1, source_target_pairs={{0,6},{1,7},{2,0},{3,1},{4,2},{5,3},{6,4},{7,5},{8,14},{9,15},{10,... | collective-permute-start | bytes 405512 | tf_op jit(solution)/shard_map/ppermute | solution.py:285
  181.7 1.6 collective-permute-start.23

commit v3 on v2

--- a/solution.py
+++ b/solution.py
@@ -115,7 +115,7 @@
     return own_ref[TILES]
 
 
-def first_kernel(a_hbm, b_hbm, out_ref, both_ref, high_ref, low_ref, a_ref, b_ref, sems):
+def first_kernel(a_hbm, b_hbm, out2_ref, out1_ref, out3_ref, both_ref, high_ref, low_ref, a_ref, b_ref, sems):
     copies = [pltpu.make_async_copy(b_hbm, b_ref, sems.at[PIECES])]
     for i in range(PIECES):
         rows = pl.ds(i * PIECE, PIECE)
@@ -132,18 +132,15 @@
         high_ref[rows, :] = a_high
         low_ref[rows, :] = a_low
     both_ref[...] = both
-    _, at = quarter(2)
-    put_half(out_ref, product(both, high, high_ref[:, at], low_ref[:, at]))
-
-
-def first_more_kernel(shift, both_ref, high_ref, low_ref, out_ref):
+    for shift, out_ref in zip(SENT, (out2_ref, out1_ref, out3_ref)):
+        _, at = quarter(shift)
+        put_half(out_ref, product(both, high, high_ref[:, at], low_ref[:, at]))
+
+
+def first_last_kernel(both_ref, high_ref, low_ref, out_ref, high_t_ref, low_t_ref):
     both = both_ref[...]
-    _, at = quarter(shift)
+    _, at = quarter(0)
     put_half(out_ref, product(both, both[:T], high_ref[:, at], low_ref[:, at]))
-
-
-def first_last_kernel(both_ref, high_ref, low_ref, out_ref, high_t_ref, low_t_ref):
-    first_more_kernel(0, both_ref, high_ref, low_ref, out_ref)
     for rows in (slice(i, i + PIECE) for i in range(0, S, PIECE)):
         for columns in (slice(i, i + PIECE) for i in range(0, F, PIECE)):
             high_t_ref[columns, rows] = high_ref[rows, columns].T
@@ -157,9 +154,9 @@
     return pl.pallas_call(
         first_kernel,
         in_specs=[anywhere, anywhere],
-        out_specs=[VMEM] * 4,
+        out_specs=[VMEM] * 6,
         out_shape=[
-            pltpu.VMEM(*QUARTER),
+            *[pltpu.VMEM(*QUARTER) for _ in SENT],
             pltpu.VMEM((2 * T, S), bf16),
             pltpu.VMEM((S, F), bf16),
             pltpu.VMEM((S, F), bf16),
@@ -383,8 +380,9 @@
 
 def gram_kernel(u_ref, other2_ref, tile_ref, out_ref):
     tile = tile_ref[...] + gram_rows(False, u_ref, other2_ref)
+    line = jnp.concatenate([tile[i : i + 1, :T] for i in range(8)], axis=1)
     for i in range(out_ref.shape[0]):
-        out_ref[i] = tile
+        out_ref[i] = line
 
 
 def solve(gram, dots, square0, ridge):
@@ -421,10 +419,12 @@
     gram = gram_ref[0]
     for i in range(1, gram_ref.shape[0]):
         gram = gram + gram_ref[i]
+    blank = jnp.zeros((1, 128 - T), f32)
+    gram = [jnp.concatenate([gram[:, i * T : (i + 1) * T], blank], axis=1) for i in range(6)]
     dots = tile_in(own2_ref) + tile_in(other2_ref)
     row = lambda tile, i: tile[i : i + 1, :]
     coefficients = solve(
-        [row(gram, i) for i in range(6)],
+        gram,
         [row(dots, i) for i in range(6)],
         row(tile_in(own0_ref), 0),
         jnp.concatenate([ridge_ref[...], jnp.zeros((1, 128 - T), f32)], axis=1),
@@ -450,11 +450,8 @@
 
 def per_device(features, targets, ridge):
     b_t = targets.T
-    parts = {}
-    parts[2], both, a_high, a_low = first(features, b_t)
-    for k in (1, 3):
-        kernel = functools.partial(first_more_kernel, k)
-        (parts[k],) = call(kernel, [QUARTER], "first_more")(both, a_high, a_low)
+    *sent, both, a_high, a_low = first(features, b_t)
+    parts = dict(zip(SENT, sent))
     outs = [QUARTER, ((F, S), bf16), ((F, S), bf16)]
     parts[0], *turned = call(first_last_kernel, outs, "first_last")(both, a_high, a_low)
     (g,) = sum_over_samp(parts)
@@ -478,7 +475,7 @@
     outs = [((2, T, F), f32), ((2, T, S), f32)]
     e, u = call(basis_kernel, outs, "basis")(*basis, other0, other1)
     (tile,) = call(gram_own_kernel, [((8, 128), f32)], "gram_own")(u, own2)
-    (tiles,) = call(gram_kernel, [((N, 8, 128), f32)], "gram")(u, other2, tile)
+    (tiles,) = call(gram_kernel, [((N, 1, 8 * T), f32)], "gram")(u, other2, tile)
     gram = lax.all_to_all(tiles, "samp", 0, 0)
     x, r = last(gram, ridge.reshape(1, T), b_t, e, q, u, own0, own2, other2)
     return x.T, r.T

time: 198 us -> 197 us (level)
    pallas_call x30 -> x28, Pallas kernels: 14.4 us -> 13.6 us  [run(): pl.pallas_call(kernel, in_specs=[VMEM] * len(args), out_specs=[VMEM] * le...]
where the time goes in v3:
time: 197 us
  blocking collectives  99.4 us (50%)
  starting transfers between devices  46.5 us (24%)
  waiting for transfers between devices  30.1 us (15%)
  Pallas kernels  20.1 us (10%)
    all_to_all x3, blocking collectives, sum_over_samp(): return (lax.all_to_all(part, 'samp', 0, 0), *tile)  49.3 us
    all_to_all x3, blocking collectives, sum_over_samp(): got = lax.all_to_all(part, 'samp', 0, 0, axis_index_groups=GROUPS_Z)  37.6 us
    ppermute x9, waiting for transfers between devices, add_over_feat(): got = [lax.ppermute(part, 'feat', shift) for shift in Y_SHIFTS]  15.1 us
    ppermute x9, starting transfers between devices, add_over_feat(): got = [lax.ppermute(part, 'feat', shift) for shift in Y_SHIFTS]  14.5 us
    ppermute x9, waiting for transfers between devices, sum_over_samp(): got = [lax.ppermute(parts[k], 'samp', X_SHIFTS[k]) for k in (3, 1, 2)]  14.4 us
    pallas_call x28, Pallas kernels, run(): pl.pallas_call(kernel, in_specs=[VMEM] * len(args), out_specs=[VMEM] * le...  13.6 us
    all_to_all x1, blocking collectives, per_device(): gram = lax.all_to_all(tiles, 'samp', 0, 0)  12.6 us
    ppermute x2, starting transfers between devices, sum_over_feat(): got = lax.ppermute(send, 'feat', CORE_SWAP)  11.9 us
  transfers between devices with their start and end apart: 24, of which 16 were waited for; matrix products, arithmetic and copies ran while one was open for 0% of the time, Pallas kernels for 4%

profile of v3, /device:TPU:1, one launch (start us, length us, event | category | flops | bytes accessed | tf_op | source)
XLA Modules:
  0.0 197.1 jit_solution(15378323037040009771)
XLA Ops:
  0.6 5.2 %first.1 = (f32[32,8,128]{2,1,0:T(8,128)S(1)}, f32[32,8,128]{2,1,0:T(8,128)S(1)}, f32[32,8,128]{2,1,0:T(8,128)S(1)}, bf16[128,1024]{1,0:T(8,128)(2,1)S(1)}, bf16...) custom-call(f32[1024,2048]{1,0:T(8,128)} %a_hbm.1, f32[64,1024]{1,0:T(8,128)} %bitcast.4), custom_call_target="tpu_custom_call" | custom-call | tf_op jit(solution)/shard_map/first/pallas_call | solution.py:154
  5.9 3.4 %collective-permute-start = (f32[32,8,128]{2,1,0:T(8,128)S(1)}, f32[32,8,128]{2,1,0:T(8,128)S(1)}, u32[]{:S(2)}, u32[]{:S(2)}) collective-permute-start(f32[32,8,128]{2,1,0:T(8,128)S(1)} %get-tuple-element.39), channel_id=1, source_target_pairs={{0,24},{8,0},{16,8},{24,16},{32,56},{40,32},{48,40},{56,48},{64,88... | collective-permute-start | bytes 393224 | tf_op jit(solution)/shard_map/ppermute | solution.py:205
  9.3 1.7 collective-permute-start.2
  11.0 2.5 %first_last.1 = (f32[32,8,128]{2,1,0:T(8,128)S(1)}, bf16[2048,1024]{1,0:T(8,128)(2,1)S(1)}, bf16[2048,1024]{1,0:T(8,128)(2,1)S(1)}) custom-call(bf16[128,1024]{1,0:T(8,128)(2,1)S(1)} %get-tuple-element.35.both_ref, bf16[1024,2048]{1,0:T(8,128)(2,1)S(1)} %get-tuple-element.36.high_ref, bf16[1024,2048]{1,0:T(8,128)(2,1)S(1)} %get-tuple-element.37.low_ref), custom_call_target="tpu_custom_call" | custom-call | tf_op jit(solution)/shard_map/first_last/pallas_call | solution.py:39
  13.5 3.2 %collective-permute-done.1.refs_2_ = f32[32,8,128]{2,1,0:T(8,128)S(1)} collective-permute-done((f32[32,8,128]{2,1,0:T(8,128)S(1)}, f32[32,8,128]{2,1,0:T(8,128)S(1)}, u32[]{:S(2)}, u32[]{:S(2)}) %collective-permute-start.1) | collective-permute-done | bytes 131104 | tf_op jit(solution)/shard_map/ppermute | solution.py:205
  16.7 16.0 %all_to_all.35.in_ref = f32[8,4,8,128]{3,2,1,0:T(8,128)S(1)} all-to-all(f32[8,4,8,128]{3,2,1,0:T(8,128)S(1)} %sum_x.3), channel_id=1, replica_groups={{0,32,64,96,128,160,192,224},{8,40,72,104,136,168,200,232},{16,48,80,11..., dimensions={0} | all-to-all | bytes 262144 | tf_op jit(solution)/shard_map/all_to_all | solution.py:207
  32.7 15.9 %all_to_all.36.g_ref = f32[32,8,512]{2,1,0:T(8,128)S(1)} all-to-all(f32[32,8,512]{2,1,0:T(8,128)S(1)} %sum_z.3), channel_id=1, replica_groups=mesh['samp'=32,'feat'=8] {'samp'}, dimensions={0} | all-to-all | bytes 1048576 | tf_op jit(solution)/shard_map/all_to_all | solution.py:210
  49.5 6.2 %collective-permute-start.3 = (f32[33,8,128]{2,1,0:T(8,128)S(1)}, f32[33,8,128]{2,1,0:T(8,128)S(1)}, u32[]{:S(2)}, u32[]{:S(2)}) collective-permute-start(f32[33,8,128]{2,1,0:T(8,128)S(1)} %get-tuple-element.45.send_ref), channel_id=1, source_target_pairs={{0,1},{1,0},{2,3},{3,2},{4,5},{5,4},{6,7},{7,6},{8,9},{9,8},{10,11... | collective-permute-start | bytes 405512 | tf_op jit(solution)/shard_map/ppermute | solution.py:275
  56.7 3.0 %collective-permute-start.6 = (f32[33,8,128]{2,1,0:T(8,128)S(1)}, f32[33,8,128]{2,1,0:T(8,128)S(1)}, u32[]{:S(2)}, u32[]{:S(2)}) collective-permute-start(f32[33,8,128]{2,1,0:T(8,128)S(1)} %add.3.refs_0_), channel_id=1, source_target_pairs={{0,4},{1,5},{2,6},{3,7},{4,0},{5,1},{6,2},{7,3},{8,12},{9,13},{10,... | collective-permute-start | bytes 405512 | tf_op jit(solution)/shard_map/ppermute | solution.py:282
  60.1 2.3 %collective-permute-start.4 = (f32[33,8,128]{2,1,0:T(8,128)S(1)}, f32[33,8,128]{2,1,0:T(8,128)S(1)}, u32[]{:S(2)}, u32[]{:S(2)}) collective-permute-start(f32[33,8,128]{2,1,0:T(8,128)S(1)} %add.3.refs_0_), channel_id=1, source_target_pairs={{0,6},{1,7},{2,0},{3,1},{4,2},{5,3},{6,4},{7,5},{8,14},{9,15},{10,... | collective-permute-start | bytes 405512 | tf_op jit(solution)/shard_map/ppermute | solution.py:282
  63.1 3.4 %collective-permute-done.5.refs_2_ = f32[33,8,128]{2,1,0:T(8,128)S(1)} collective-permute-done((f32[33,8,128]{2,1,0:T(8,128)S(1)}, f32[33,8,128]{2,1,0:T(8,128)S(1)}, u32[]{:S(2)}, u32[]{:S(2)}) %collective-permute-start.5) | collective-permute-done | bytes 135200 | tf_op jit(solution)/shard_map/ppermute | solution.py:282
  69.6 1.6 collective-permute-start.8
  71.2 1.8 collective-permute-start.10
  74.4 3.7 %collective-permute-done.9.refs_2_ = f32[32,8,128]{2,1,0:T(8,128)S(1)} collective-permute-done((f32[32,8,128]{2,1,0:T(8,128)S(1)}, f32[32,8,128]{2,1,0:T(8,128)S(1)}, u32[]{:S(2)}, u32[]{:S(2)}) %collective-permute-start.9) | collective-permute-done | bytes 131104 | tf_op jit(solution)/shard_map/ppermute | solution.py:205
  78.7 10.7 %all_to_all.37.in_ref = f32[8,4,8,128]{3,2,1,0:T(8,128)S(1)} all-to-all(f32[8,4,8,128]{3,2,1,0:T(8,128)S(1)} %sum_x.4), channel_id=1, replica_groups={{0,32,64,96,128,160,192,224},{8,40,72,104,136,168,200,232},{16,48,80,11..., dimensions={0} | all-to-all | bytes 262144 | tf_op jit(solution)/shard_map/all_to_all | solution.py:207
  89.5 16.5 %all_to_all.38.w_ref.w1_ref = f32[32,8,512]{2,1,0:T(8,128)S(1)} all-to-all(f32[32,8,512]{2,1,0:T(8,128)S(1)} %sum_z.4), channel_id=1, replica_groups=mesh['samp'=32,'feat'=8] {'samp'}, dimensions={0} | all-to-all | bytes 1048576 | tf_op jit(solution)/shard_map/all_to_all | solution.py:210
  106.9 5.6 %collective-permute-start.11 = (f32[33,8,128]{2,1,0:T(8,128)S(1)}, f32[33,8,128]{2,1,0:T(8,128)S(1)}, u32[]{:S(2)}, u32[]{:S(2)}) collective-permute-start(f32[33,8,128]{2,1,0:T(8,128)S(1)} %get-tuple-element.51.send_ref), channel_id=1, source_target_pairs={{0,1},{1,0},{2,3},{3,2},{4,5},{5,4},{6,7},{7,6},{8,9},{9,8},{10,11... | collective-permute-start | bytes 405512 | tf_op jit(solution)/shard_map/ppermute | solution.py:275
  113.6 1.9 collective-permute-start.14
  115.4 1.4 collective-permute-start.13
  118.1 1.9 collective-permute-done.14.refs_3_
  120.0 3.5 %collective-permute-done.13.refs_2_ = f32[33,8,128]{2,1,0:T(8,128)S(1)} collective-permute-done((f32[33,8,128]{2,1,0:T(8,128)S(1)}, f32[33,8,128]{2,1,0:T(8,128)S(1)}, u32[]{:S(2)}, u32[]{:S(2)}) %collective-permute-start.13) | collective-permute-done | bytes 135200 | tf_op jit(solution)/shard_map/ppermute | solution.py:282
  126.4 1.5 collective-permute-start.16
  128.0 1.7 collective-permute-start.18
  129.9 1.5 collective-permute-done.16.refs_1_
  131.4 3.3 %collective-permute-done.17.refs_2_ = f32[33,8,128]{2,1,0:T(8,128)S(1)} collective-permute-done((f32[33,8,128]{2,1,0:T(8,128)S(1)}, f32[33,8,128]{2,1,0:T(8,128)S(1)}, u32[]{:S(2)}, u32[]{:S(2)}) %collective-permute-start.17) | collective-permute-done | bytes 135200 | tf_op jit(solution)/shard_map/ppermute | solution.py:205
  135.7 10.9 %all_to_all.39.in_ref = f32[8,5,8,128]{3,2,1,0:T(8,128)S(1)} all-to-all(f32[8,5,8,128]{3,2,1,0:T(8,128)S(1)} %sum_x.5), channel_id=1, replica_groups={{0,32,64,96,128,160,192,224},{8,40,72,104,136,168,200,232},{16,48,80,11..., dimensions={0} | all-to-all | bytes 327680 | tf_op jit(solution)/shard_map/all_to_all | solution.py:207
  146.6 16.8 %all_to_all.40.w_ref = f32[32,8,512]{2,1,0:T(8,128)S(1)} all-to-all(f32[32,8,512]{2,1,0:T(8,128)S(1)} %get-tuple-element.60), channel_id=1, replica_groups=mesh['samp'=32,'feat'=8] {'samp'}, dimensions={0} | all-to-all | bytes 1048576 | tf_op jit(solution)/shard_map/all_to_all | solution.py:210
  164.6 5.6 %collective-permute-start.19 = (f32[33,8,128]{2,1,0:T(8,128)S(1)}, f32[33,8,128]{2,1,0:T(8,128)S(1)}, u32[]{:S(2)}, u32[]{:S(2)}) collective-permute-start(f32[33,8,128]{2,1,0:T(8,128)S(1)} %get-tuple-element.64), channel_id=1, source_target_pairs={{0,1},{1,0},{2,3},{3,2},{4,5},{5,4},{6,7},{7,6},{8,9},{9,8},{10,11... | collective-permute-start | bytes 405512 | tf_op jit(solution)/shard_map/ppermute | solution.py:472
  171.3 1.7 collective-permute-start.22
  175.7 2.2 %collective-permute-done.22.refs_3_ = f32[33,8,128]{2,1,0:T(8,128)S(1)} collective-permute-done((f32[33,8,128]{2,1,0:T(8,128)S(1)}, f32[33,8,128]{2,1,0:T(8,128)S(1)}, u32[]{:S(2)}, u32[]{:S(2)}) %collective-permute-start.22) | collective-permute-done | bytes 135200 | tf_op jit(solution)/shard_map/ppermute | solution.py:282
  177.8 3.5 %collective-permute-done.21.refs_2_ = f32[33,8,128]{2,1,0:T(8,128)S(1)} collective-permute-done((f32[33,8,128]{2,1,0:T(8,128)S(1)}, f32[33,8,128]{2,1,0:T(8,128)S(1)}, u32[]{:S(2)}, u32[]{:S(2)}) %collective-permute-start.21) | collective-permute-done | bytes 135200 | tf_op jit(solution)/shard_map/ppermute | solution.py:282
  183.2 12.6 %all_to_all.41.gram_ref = f32[32,1,512]{2,1,0:T(1,128)S(1)} all-to-all(f32[32,1,512]{2,1,0:T(1,128)S(1)} %gram.1), channel_id=1, replica_groups=mesh['samp'=32,'feat'=8] {'samp'}, dimensions={0} | all-to-all | bytes 131072 | tf_op jit(solution)/shard_map/all_to_all | solution.py:479
  (57 shorter events, 23.9 us)
Async XLA Ops:
  5.9 7.6 %collective-permute-start = (f32[32,8,128]{2,1,0:T(8,128)S(1)}, f32[32,8,128]{2,1,0:T(8,128)S(1)}, u32[]{:S(2)}, u32[]{:S(2)}) collective-permute-start(f32[32,8,128]{2,1,0:T(8,128)S(1)} %get-tuple-element.39), channel_id=1, source_target_pairs={{0,24},{8,0},{16,8},{24,16},{32,56},{40,32},{48,40},{56,48},{64,88... | collective-permute-start | bytes 393224 | tf_op jit(solution)/shard_map/ppermute | solution.py:205
  9.3 7.4 %collective-permute-start.1 = (f32[32,8,128]{2,1,0:T(8,128)S(1)}, f32[32,8,128]{2,1,0:T(8,128)S(1)}, u32[]{:S(2)}, u32[]{:S(2)}) collective-permute-start(f32[32,8,128]{2,1,0:T(8,128)S(1)} %get-tuple-element.40), channel_id=1, source_target_pairs={{0,8},{8,16},{16,24},{24,0},{32,40},{40,48},{48,56},{56,32},{64,72... | collective-permute-start | bytes 393224 | tf_op jit(solution)/shard_map/ppermute | solution.py:205
  9.3 7.4 %collective-permute-start.2 = (f32[32,8,128]{2,1,0:T(8,128)S(1)}, f32[32,8,128]{2,1,0:T(8,128)S(1)}, u32[]{:S(2)}, u32[]{:S(2)}) collective-permute-start(f32[32,8,128]{2,1,0:T(8,128)S(1)} %get-tuple-element.41), channel_id=1, source_target_pairs={{0,16},{8,24},{16,0},{24,8},{32,48},{40,56},{48,32},{56,40},{64,80... | collective-permute-start | bytes 393224 | tf_op jit(solution)/shard_map/ppermute | solution.py:205
  49.5 7.2 %collective-permute-start.3 = (f32[33,8,128]{2,1,0:T(8,128)S(1)}, f32[33,8,128]{2,1,0:T(8,128)S(1)}, u32[]{:S(2)}, u32[]{:S(2)}) collective-permute-start(f32[33,8,128]{2,1,0:T(8,128)S(1)} %get-tuple-element.45.send_ref), channel_id=1, source_target_pairs={{0,1},{1,0},{2,3},{3,2},{4,5},{5,4},{6,7},{7,6},{8,9},{9,8},{10,11... | collective-permute-start | bytes 405512 | tf_op jit(solution)/shard_map/ppermute | solution.py:275
  56.7 6.4 %collective-permute-start.6 = (f32[33,8,128]{2,1,0:T(8,128)S(1)}, f32[33,8,128]{2,1,0:T(8,128)S(1)}, u32[]{:S(2)}, u32[]{:S(2)}) collective-permute-start(f32[33,8,128]{2,1,0:T(8,128)S(1)} %add.3.refs_0_), channel_id=1, source_target_pairs={{0,4},{1,5},{2,6},{3,7},{4,0},{5,1},{6,2},{7,3},{8,12},{9,13},{10,... | collective-permute-start | bytes 405512 | tf_op jit(solution)/shard_map/ppermute | solution.py:282
  59.7 6.8 %collective-permute-start.5 = (f32[33,8,128]{2,1,0:T(8,128)S(1)}, f32[33,8,128]{2,1,0:T(8,128)S(1)}, u32[]{:S(2)}, u32[]{:S(2)}) collective-permute-start(f32[33,8,128]{2,1,0:T(8,128)S(1)} %add.3.refs_0_), channel_id=1, source_target_pairs={{0,2},{1,3},{2,4},{3,5},{4,6},{5,7},{6,0},{7,1},{8,10},{9,11},{10,... | collective-permute-start | bytes 405512 | tf_op jit(solution)/shard_map/ppermute | solution.py:282
  60.1 6.4 %collective-permute-start.4 = (f32[33,8,128]{2,1,0:T(8,128)S(1)}, f32[33,8,128]{2,1,0:T(8,128)S(1)}, u32[]{:S(2)}, u32[]{:S(2)}) collective-permute-start(f32[33,8,128]{2,1,0:T(8,128)S(1)} %add.3.refs_0_), channel_id=1, source_target_pairs={{0,6},{1,7},{2,0},{3,1},{4,2},{5,3},{6,4},{7,5},{8,14},{9,15},{10,... | collective-permute-start | bytes 405512 | tf_op jit(solution)/shard_map/ppermute | solution.py:282
  66.5 2.3 %collective-permute-start.7 = (f32[33,8,128]{2,1,0:T(8,128)S(1)}, f32[33,8,128]{2,1,0:T(8,128)S(1)}, u32[]{:S(2)}, u32[]{:S(2)}) collective-permute-start(f32[33,8,128]{2,1,0:T(8,128)S(1)} %sum_y.3.own0_ref), channel_id=1, source_target_pairs={{0,1},{1,0},{2,3},{3,2},{4,5},{5,4},{6,7},{7,6},{8,9},{9,8},{10,11... | collective-permute-start | bytes 405512 | tf_op jit(solution)/shard_map/ppermute | solution.py:284
  69.6 4.8 %collective-permute-start.8 = (f32[32,8,128]{2,1,0:T(8,128)S(1)}, f32[32,8,128]{2,1,0:T(8,128)S(1)}, u32[]{:S(2)}, u32[]{:S(2)}) collective-permute-start(f32[32,8,128]{2,1,0:T(8,128)S(1)} %get-tuple-element.47), channel_id=1, source_target_pairs={{0,24},{8,0},{16,8},{24,16},{32,56},{40,32},{48,40},{56,48},{64,88... | collective-permute-start | bytes 393224 | tf_op jit(solution)/shard_map/ppermute | solution.py:205
  71.2 6.8 %collective-permute-start.9 = (f32[32,8,128]{2,1,0:T(8,128)S(1)}, f32[32,8,128]{2,1,0:T(8,128)S(1)}, u32[]{:S(2)}, u32[]{:S(2)}) collective-permute-start(f32[32,8,128]{2,1,0:T(8,128)S(1)} %get-tuple-element.48), channel_id=1, source_target_pairs={{0,8},{8,16},{16,24},{24,0},{32,40},{40,48},{48,56},{56,32},{64,72... | collective-permute-start | bytes 393224 | tf_op jit(solution)/shard_map/ppermute | solution.py:205
  71.2 7.5 %collective-permute-start.10 = (f32[32,8,128]{2,1,0:T(8,128)S(1)}, f32[32,8,128]{2,1,0:T(8,128)S(1)}, u32[]{:S(2)}, u32[]{:S(2)}) collective-permute-start(f32[32,8,128]{2,1,0:T(8,128)S(1)} %get-tuple-element.49), channel_id=1, source_target_pairs={{0,16},{8,24},{16,0},{24,8},{32,48},{40,56},{48,32},{56,40},{64,80... | collective-permute-start | bytes 393224 | tf_op jit(solution)/shard_map/ppermute | solution.py:205
  106.9 6.6 %collective-permute-start.11 = (f32[33,8,128]{2,1,0:T(8,128)S(1)}, f32[33,8,128]{2,1,0:T(8,128)S(1)}, u32[]{:S(2)}, u32[]{:S(2)}) collective-permute-start(f32[33,8,128]{2,1,0:T(8,128)S(1)} %get-tuple-element.51.send_ref), channel_id=1, source_target_pairs={{0,1},{1,0},{2,3},{3,2},{4,5},{5,4},{6,7},{7,6},{8,9},{9,8},{10,11... | collective-permute-start | bytes 405512 | tf_op jit(solution)/shard_map/ppermute | solution.py:275
  113.6 6.4 %collective-permute-start.14 = (f32[33,8,128]{2,1,0:T(8,128)S(1)}, f32[33,8,128]{2,1,0:T(8,128)S(1)}, u32[]{:S(2)}, u32[]{:S(2)}) collective-permute-start(f32[33,8,128]{2,1,0:T(8,128)S(1)} %add.4.refs_0_), channel_id=1, source_target_pairs={{0,4},{1,5},{2,6},{3,7},{4,0},{5,1},{6,2},{7,3},{8,12},{9,13},{10,... | collective-permute-start | bytes 405512 | tf_op jit(solution)/shard_map/ppermute | solution.py:282
  115.4 8.0 %collective-permute-start.13 = (f32[33,8,128]{2,1,0:T(8,128)S(1)}, f32[33,8,128]{2,1,0:T(8,128)S(1)}, u32[]{:S(2)}, u32[]{:S(2)}) collective-permute-start(f32[33,8,128]{2,1,0:T(8,128)S(1)} %add.4.refs_0_), channel_id=1, source_target_pairs={{0,2},{1,3},{2,4},{3,5},{4,6},{5,7},{6,0},{7,1},{8,10},{9,11},{10,... | collective-permute-start | bytes 405512 | tf_op jit(solution)/shard_map/ppermute | solution.py:282
  116.8 6.6 %collective-permute-start.12 = (f32[33,8,128]{2,1,0:T(8,128)S(1)}, f32[33,8,128]{2,1,0:T(8,128)S(1)}, u32[]{:S(2)}, u32[]{:S(2)}) collective-permute-start(f32[33,8,128]{2,1,0:T(8,128)S(1)} %add.4.refs_0_), channel_id=1, source_target_pairs={{0,6},{1,7},{2,0},{3,1},{4,2},{5,3},{6,4},{7,5},{8,14},{9,15},{10,... | collective-permute-start | bytes 405512 | tf_op jit(solution)/shard_map/ppermute | solution.py:282
  123.5 2.0 %collective-permute-start.15 = (f32[33,8,128]{2,1,0:T(8,128)S(1)}, f32[33,8,128]{2,1,0:T(8,128)S(1)}, u32[]{:S(2)}, u32[]{:S(2)}) collective-permute-start(f32[33,8,128]{2,1,0:T(8,128)S(1)} %sum_y.4.own1_ref), channel_id=1, source_target_pairs={{0,1},{1,0},{2,3},{3,2},{4,5},{5,4},{6,7},{7,6},{8,9},{9,8},{10,11... | collective-permute-start | bytes 405512 | tf_op jit(solution)/shard_map/ppermute | solution.py:284
  126.4 5.0 %collective-permute-start.16 = (f32[33,8,128]{2,1,0:T(8,128)S(1)}, f32[33,8,128]{2,1,0:T(8,128)S(1)}, u32[]{:S(2)}, u32[]{:S(2)}) collective-permute-start(f32[33,8,128]{2,1,0:T(8,128)S(1)} %get-tuple-element.57), channel_id=1, source_target_pairs={{0,24},{8,0},{16,8},{24,16},{32,56},{40,32},{48,40},{56,48},{64,88... | collective-permute-start | bytes 405512 | tf_op jit(solution)/shard_map/ppermute | solution.py:205
  127.9 6.8 %collective-permute-start.17 = (f32[33,8,128]{2,1,0:T(8,128)S(1)}, f32[33,8,128]{2,1,0:T(8,128)S(1)}, u32[]{:S(2)}, u32[]{:S(2)}) collective-permute-start(f32[33,8,128]{2,1,0:T(8,128)S(1)} %get-tuple-element.58), channel_id=1, source_target_pairs={{0,8},{8,16},{16,24},{24,0},{32,40},{40,48},{48,56},{56,32},{64,72... | collective-permute-start | bytes 405512 | tf_op jit(solution)/shard_map/ppermute | solution.py:205
  128.0 7.7 %collective-permute-start.18 = (f32[33,8,128]{2,1,0:T(8,128)S(1)}, f32[33,8,128]{2,1,0:T(8,128)S(1)}, u32[]{:S(2)}, u32[]{:S(2)}) collective-permute-start(f32[33,8,128]{2,1,0:T(8,128)S(1)} %get-tuple-element.59), channel_id=1, source_target_pairs={{0,16},{8,24},{16,0},{24,8},{32,48},{40,56},{48,32},{56,40},{64,80... | collective-permute-start | bytes 405512 | tf_op jit(solution)/shard_map/ppermute | solution.py:205
  164.6 6.7 %collective-permute-start.19 = (f32[33,8,128]{2,1,0:T(8,128)S(1)}, f32[33,8,128]{2,1,0:T(8,128)S(1)}, u32[]{:S(2)}, u32[]{:S(2)}) collective-permute-start(f32[33,8,128]{2,1,0:T(8,128)S(1)} %get-tuple-element.64), channel_id=1, source_target_pairs={{0,1},{1,0},{2,3},{3,2},{4,5},{5,4},{6,7},{7,6},{8,9},{9,8},{10,11... | collective-permute-start | bytes 405512 | tf_op jit(solution)/shard_map/ppermute | solution.py:472
  171.3 24.5 %copy-start = (f32[1024,64]{0,1:T(8,128)S(1)}, f32[1024,64]{0,1:T(8,128)}, u32[]{:S(2)}) copy-start(f32[1024,64]{0,1:T(8,128)} %param.4) | copy-start | bytes 786436
  171.3 24.5 %copy-start.1 = (f32[64]{0:T(128)S(1)}, f32[64]{0:T(128)}, u32[]{:S(2)}) copy-start(f32[64]{0:T(128)} %param.5) | copy-start | bytes 772
  171.3 6.5 %collective-permute-start.22 = (f32[33,8,128]{2,1,0:T(8,128)S(1)}, f32[33,8,128]{2,1,0:T(8,128)S(1)}, u32[]{:S(2)}, u32[]{:S(2)}) collective-permute-start(f32[33,8,128]{2,1,0:T(8,128)S(1)} %add.5.refs_0_), channel_id=1, source_target_pairs={{0,4},{1,5},{2,6},{3,7},{4,0},{5,1},{6,2},{7,3},{8,12},{9,13},{10,... | collective-permute-start | bytes 405512 | tf_op jit(solution)/shard_map/ppermute | solution.py:282
  173.0 8.3 %collective-permute-start.21 = (f32[33,8,128]{2,1,0:T(8,128)S(1)}, f32[33,8,128]{2,1,0:T(8,128)S(1)}, u32[]{:S(2)}, u32[]{:S(2)}) collective-permute-start(f32[33,8,128]{2,1,0:T(8,128)S(1)} %add.5.refs_0_), channel_id=1, source_target_pairs={{0,2},{1,3},{2,4},{3,5},{4,6},{5,7},{6,0},{7,1},{8,10},{9,11},{10,... | collective-permute-start | bytes 405512 | tf_op jit(solution)/shard_map/ppermute | solution.py:282
  174.4 6.9 %collective-permute-start.20 = (f32[33,8,128]{2,1,0:T(8,128)S(1)}, f32[33,8,128]{2,1,0:T(8,128)S(1)}, u32[]{:S(2)}, u32[]{:S(2)}) collective-permute-start(f32[33,8,128]{2,1,0:T(8,128)S(1)} %add.5.refs_0_), channel_id=1, source_target_pairs={{0,6},{1,7},{2,0},{3,1},{4,2},{5,3},{6,4},{7,5},{8,14},{9,15},{10,... | collective-permute-start | bytes 405512 | tf_op jit(solution)/shard_map/ppermute | solution.py:282
  181.4 1.6 collective-permute-start.23

commit v4 on v3

--- a/solution.py
+++ b/solution.py
@@ -380,7 +380,7 @@
 
 def gram_kernel(u_ref, other2_ref, tile_ref, out_ref):
     tile = tile_ref[...] + gram_rows(False, u_ref, other2_ref)
-    line = jnp.concatenate([tile[i : i + 1, :T] for i in range(8)], axis=1)
+    line = jnp.concatenate([tile[i : i + 1, :T] for i in range(len(PAIRS))], axis=1)
     for i in range(out_ref.shape[0]):
         out_ref[i] = line
 
@@ -475,7 +475,7 @@
     outs = [((2, T, F), f32), ((2, T, S), f32)]
     e, u = call(basis_kernel, outs, "basis")(*basis, other0, other1)
     (tile,) = call(gram_own_kernel, [((8, 128), f32)], "gram_own")(u, own2)
-    (tiles,) = call(gram_kernel, [((N, 1, 8 * T), f32)], "gram")(u, other2, tile)
+    (tiles,) = call(gram_kernel, [((N, 1, len(PAIRS) * T), f32)], "gram")(u, other2, tile)
     gram = lax.all_to_all(tiles, "samp", 0, 0)
     x, r = last(gram, ridge.reshape(1, T), b_t, e, q, u, own0, own2, other2)
     return x.T, r.T

time: 197 us -> 197 us (level)
  no operation moved by 1% of the time
where the time goes in v4:
time: 197 us
  blocking collectives  99.4 us (50%)
  starting transfers between devices  46.5 us (24%)
  waiting for transfers between devices  30.1 us (15%)
  Pallas kernels  20.1 us (10%)
    all_to_all x3, blocking collectives, sum_over_samp(): return (lax.all_to_all(part, 'samp', 0, 0), *tile)  49.3 us
    all_to_all x3, blocking collectives, sum_over_samp(): got = lax.all_to_all(part, 'samp', 0, 0, axis_index_groups=GROUPS_Z)  37.6 us
    ppermute x9, waiting for transfers between devices, add_over_feat(): got = [lax.ppermute(part, 'feat', shift) for shift in Y_SHIFTS]  15.1 us
    ppermute x9, starting transfers between devices, add_over_feat(): got = [lax.ppermute(part, 'feat', shift) for shift in Y_SHIFTS]  14.5 us
    ppermute x9, waiting for transfers between devices, sum_over_samp(): got = [lax.ppermute(parts[k], 'samp', X_SHIFTS[k]) for k in (3, 1, 2)]  14.4 us
    pallas_call x28, Pallas kernels, run(): pl.pallas_call(kernel, in_specs=[VMEM] * len(args), out_specs=[VMEM] * le...  13.6 us
    all_to_all x1, blocking collectives, per_device(): gram = lax.all_to_all(tiles, 'samp', 0, 0)  12.5 us
    ppermute x2, starting transfers between devices, sum_over_feat(): got = lax.ppermute(send, 'feat', CORE_SWAP)  11.9 us
  transfers between devices with their start and end apart: 24, of which 16 were waited for; matrix products, arithmetic and copies ran while one was open for 0% of the time, Pallas kernels for 4%

profile of v4, /device:TPU:1, one launch (start us, length us, event | category | flops | bytes accessed | tf_op | source)
XLA Modules:
  0.0 197.0 jit_solution(4497222766295577437)
XLA Ops:
  0.6 5.2 %first.1 = (f32[32,8,128]{2,1,0:T(8,128)S(1)}, f32[32,8,128]{2,1,0:T(8,128)S(1)}, f32[32,8,128]{2,1,0:T(8,128)S(1)}, bf16[128,1024]{1,0:T(8,128)(2,1)S(1)}, bf16...) custom-call(f32[1024,2048]{1,0:T(8,128)} %a_hbm.1, f32[64,1024]{1,0:T(8,128)} %bitcast.4), custom_call_target="tpu_custom_call" | custom-call | tf_op jit(solution)/shard_map/first/pallas_call | solution.py:154
  5.9 3.4 %collective-permute-start = (f32[32,8,128]{2,1,0:T(8,128)S(1)}, f32[32,8,128]{2,1,0:T(8,128)S(1)}, u32[]{:S(2)}, u32[]{:S(2)}) collective-permute-start(f32[32,8,128]{2,1,0:T(8,128)S(1)} %get-tuple-element.39), channel_id=1, source_target_pairs={{0,24},{8,0},{16,8},{24,16},{32,56},{40,32},{48,40},{56,48},{64,88... | collective-permute-start | bytes 393224 | tf_op jit(solution)/shard_map/ppermute | solution.py:205
  9.3 1.7 collective-permute-start.2
  11.0 2.5 %first_last.1 = (f32[32,8,128]{2,1,0:T(8,128)S(1)}, bf16[2048,1024]{1,0:T(8,128)(2,1)S(1)}, bf16[2048,1024]{1,0:T(8,128)(2,1)S(1)}) custom-call(bf16[128,1024]{1,0:T(8,128)(2,1)S(1)} %get-tuple-element.35.both_ref, bf16[1024,2048]{1,0:T(8,128)(2,1)S(1)} %get-tuple-element.36.high_ref, bf16[1024,2048]{1,0:T(8,128)(2,1)S(1)} %get-tuple-element.37.low_ref), custom_call_target="tpu_custom_call" | custom-call | tf_op jit(solution)/shard_map/first_last/pallas_call | solution.py:39
  13.5 3.2 %collective-permute-done.1.refs_2_ = f32[32,8,128]{2,1,0:T(8,128)S(1)} collective-permute-done((f32[32,8,128]{2,1,0:T(8,128)S(1)}, f32[32,8,128]{2,1,0:T(8,128)S(1)}, u32[]{:S(2)}, u32[]{:S(2)}) %collective-permute-start.1) | collective-permute-done | bytes 131104 | tf_op jit(solution)/shard_map/ppermute | solution.py:205
  16.7 16.0 %all_to_all.35.in_ref = f32[8,4,8,128]{3,2,1,0:T(8,128)S(1)} all-to-all(f32[8,4,8,128]{3,2,1,0:T(8,128)S(1)} %sum_x.3), channel_id=1, replica_groups={{0,32,64,96,128,160,192,224},{8,40,72,104,136,168,200,232},{16,48,80,11..., dimensions={0} | all-to-all | bytes 262144 | tf_op jit(solution)/shard_map/all_to_all | solution.py:207
  32.7 15.9 %all_to_all.36.g_ref = f32[32,8,512]{2,1,0:T(8,128)S(1)} all-to-all(f32[32,8,512]{2,1,0:T(8,128)S(1)} %sum_z.3), channel_id=1, replica_groups=mesh['samp'=32,'feat'=8] {'samp'}, dimensions={0} | all-to-all | bytes 1048576 | tf_op jit(solution)/shard_map/all_to_all | solution.py:210
  49.5 6.2 %collective-permute-start.3 = (f32[33,8,128]{2,1,0:T(8,128)S(1)}, f32[33,8,128]{2,1,0:T(8,128)S(1)}, u32[]{:S(2)}, u32[]{:S(2)}) collective-permute-start(f32[33,8,128]{2,1,0:T(8,128)S(1)} %get-tuple-element.45.send_ref), channel_id=1, source_target_pairs={{0,1},{1,0},{2,3},{3,2},{4,5},{5,4},{6,7},{7,6},{8,9},{9,8},{10,11... | collective-permute-start | bytes 405512 | tf_op jit(solution)/shard_map/ppermute | solution.py:275
  56.7 3.0 %collective-permute-start.6 = (f32[33,8,128]{2,1,0:T(8,128)S(1)}, f32[33,8,128]{2,1,0:T(8,128)S(1)}, u32[]{:S(2)}, u32[]{:S(2)}) collective-permute-start(f32[33,8,128]{2,1,0:T(8,128)S(1)} %add.3.refs_0_), channel_id=1, source_target_pairs={{0,4},{1,5},{2,6},{3,7},{4,0},{5,1},{6,2},{7,3},{8,12},{9,13},{10,... | collective-permute-start | bytes 405512 | tf_op jit(solution)/shard_map/ppermute | solution.py:282
  60.1 2.3 %collective-permute-start.4 = (f32[33,8,128]{2,1,0:T(8,128)S(1)}, f32[33,8,128]{2,1,0:T(8,128)S(1)}, u32[]{:S(2)}, u32[]{:S(2)}) collective-permute-start(f32[33,8,128]{2,1,0:T(8,128)S(1)} %add.3.refs_0_), channel_id=1, source_target_pairs={{0,6},{1,7},{2,0},{3,1},{4,2},{5,3},{6,4},{7,5},{8,14},{9,15},{10,... | collective-permute-start | bytes 405512 | tf_op jit(solution)/shard_map/ppermute | solution.py:282
  63.1 3.4 %collective-permute-done.5.refs_2_ = f32[33,8,128]{2,1,0:T(8,128)S(1)} collective-permute-done((f32[33,8,128]{2,1,0:T(8,128)S(1)}, f32[33,8,128]{2,1,0:T(8,128)S(1)}, u32[]{:S(2)}, u32[]{:S(2)}) %collective-permute-start.5) | collective-permute-done | bytes 135200 | tf_op jit(solution)/shard_map/ppermute | solution.py:282
  69.6 1.6 collective-permute-start.8
  71.2 1.8 collective-permute-start.10
  74.4 3.7 %collective-permute-done.9.refs_2_ = f32[32,8,128]{2,1,0:T(8,128)S(1)} collective-permute-done((f32[32,8,128]{2,1,0:T(8,128)S(1)}, f32[32,8,128]{2,1,0:T(8,128)S(1)}, u32[]{:S(2)}, u32[]{:S(2)}) %collective-permute-start.9) | collective-permute-done | bytes 131104 | tf_op jit(solution)/shard_map/ppermute | solution.py:205
  78.7 10.7 %all_to_all.37.in_ref = f32[8,4,8,128]{3,2,1,0:T(8,128)S(1)} all-to-all(f32[8,4,8,128]{3,2,1,0:T(8,128)S(1)} %sum_x.4), channel_id=1, replica_groups={{0,32,64,96,128,160,192,224},{8,40,72,104,136,168,200,232},{16,48,80,11..., dimensions={0} | all-to-all | bytes 262144 | tf_op jit(solution)/shard_map/all_to_all | solution.py:207
  89.5 16.5 %all_to_all.38.w_ref.w1_ref = f32[32,8,512]{2,1,0:T(8,128)S(1)} all-to-all(f32[32,8,512]{2,1,0:T(8,128)S(1)} %sum_z.4), channel_id=1, replica_groups=mesh['samp'=32,'feat'=8] {'samp'}, dimensions={0} | all-to-all | bytes 1048576 | tf_op jit(solution)/shard_map/all_to_all | solution.py:210
  106.9 5.6 %collective-permute-start.11 = (f32[33,8,128]{2,1,0:T(8,128)S(1)}, f32[33,8,128]{2,1,0:T(8,128)S(1)}, u32[]{:S(2)}, u32[]{:S(2)}) collective-permute-start(f32[33,8,128]{2,1,0:T(8,128)S(1)} %get-tuple-element.51.send_ref), channel_id=1, source_target_pairs={{0,1},{1,0},{2,3},{3,2},{4,5},{5,4},{6,7},{7,6},{8,9},{9,8},{10,11... | collective-permute-start | bytes 405512 | tf_op jit(solution)/shard_map/ppermute | solution.py:275
  113.6 1.9 collective-permute-start.14
  115.4 1.4 collective-permute-start.13
  118.1 1.9 collective-permute-done.14.refs_3_
  120.0 3.5 %collective-permute-done.13.refs_2_ = f32[33,8,128]{2,1,0:T(8,128)S(1)} collective-permute-done((f32[33,8,128]{2,1,0:T(8,128)S(1)}, f32[33,8,128]{2,1,0:T(8,128)S(1)}, u32[]{:S(2)}, u32[]{:S(2)}) %collective-permute-start.13) | collective-permute-done | bytes 135200 | tf_op jit(solution)/shard_map/ppermute | solution.py:282
  126.4 1.5 collective-permute-start.16
  128.0 1.7 collective-permute-start.18
  129.9 1.5 collective-permute-done.16.refs_1_
  131.4 3.3 %collective-permute-done.17.refs_2_ = f32[33,8,128]{2,1,0:T(8,128)S(1)} collective-permute-done((f32[33,8,128]{2,1,0:T(8,128)S(1)}, f32[33,8,128]{2,1,0:T(8,128)S(1)}, u32[]{:S(2)}, u32[]{:S(2)}) %collective-permute-start.17) | collective-permute-done | bytes 135200 | tf_op jit(solution)/shard_map/ppermute | solution.py:205
  135.7 10.9 %all_to_all.39.in_ref = f32[8,5,8,128]{3,2,1,0:T(8,128)S(1)} all-to-all(f32[8,5,8,128]{3,2,1,0:T(8,128)S(1)} %sum_x.5), channel_id=1, replica_groups={{0,32,64,96,128,160,192,224},{8,40,72,104,136,168,200,232},{16,48,80,11..., dimensions={0} | all-to-all | bytes 327680 | tf_op jit(solution)/shard_map/all_to_all | solution.py:207
  146.6 16.8 %all_to_all.40.w_ref = f32[32,8,512]{2,1,0:T(8,128)S(1)} all-to-all(f32[32,8,512]{2,1,0:T(8,128)S(1)} %get-tuple-element.60), channel_id=1, replica_groups=mesh['samp'=32,'feat'=8] {'samp'}, dimensions={0} | all-to-all | bytes 1048576 | tf_op jit(solution)/shard_map/all_to_all | solution.py:210
  164.6 5.6 %collective-permute-start.19 = (f32[33,8,128]{2,1,0:T(8,128)S(1)}, f32[33,8,128]{2,1,0:T(8,128)S(1)}, u32[]{:S(2)}, u32[]{:S(2)}) collective-permute-start(f32[33,8,128]{2,1,0:T(8,128)S(1)} %get-tuple-element.64), channel_id=1, source_target_pairs={{0,1},{1,0},{2,3},{3,2},{4,5},{5,4},{6,7},{7,6},{8,9},{9,8},{10,11... | collective-permute-start | bytes 405512 | tf_op jit(solution)/shard_map/ppermute | solution.py:472
  171.3 1.7 collective-permute-start.22
  175.7 2.1 %collective-permute-done.22.refs_3_ = f32[33,8,128]{2,1,0:T(8,128)S(1)} collective-permute-done((f32[33,8,128]{2,1,0:T(8,128)S(1)}, f32[33,8,128]{2,1,0:T(8,128)S(1)}, u32[]{:S(2)}, u32[]{:S(2)}) %collective-permute-start.22) | collective-permute-done | bytes 135200 | tf_op jit(solution)/shard_map/ppermute | solution.py:282
  177.8 3.5 %collective-permute-done.21.refs_2_ = f32[33,8,128]{2,1,0:T(8,128)S(1)} collective-permute-done((f32[33,8,128]{2,1,0:T(8,128)S(1)}, f32[33,8,128]{2,1,0:T(8,128)S(1)}, u32[]{:S(2)}, u32[]{:S(2)}) %collective-permute-start.21) | collective-permute-done | bytes 135200 | tf_op jit(solution)/shard_map/ppermute | solution.py:282
  183.2 12.5 %all_to_all.41.gram_ref = f32[32,1,384]{2,1,0:T(1,128)S(1)} all-to-all(f32[32,1,384]{2,1,0:T(1,128)S(1)} %gram.1), channel_id=1, replica_groups=mesh['samp'=32,'feat'=8] {'samp'}, dimensions={0} | all-to-all | bytes 98304 | tf_op jit(solution)/shard_map/all_to_all | solution.py:479
  (57 shorter events, 23.9 us)
Async XLA Ops:
  5.9 7.6 %collective-permute-start = (f32[32,8,128]{2,1,0:T(8,128)S(1)}, f32[32,8,128]{2,1,0:T(8,128)S(1)}, u32[]{:S(2)}, u32[]{:S(2)}) collective-permute-start(f32[32,8,128]{2,1,0:T(8,128)S(1)} %get-tuple-element.39), channel_id=1, source_target_pairs={{0,24},{8,0},{16,8},{24,16},{32,56},{40,32},{48,40},{56,48},{64,88... | collective-permute-start | bytes 393224 | tf_op jit(solution)/shard_map/ppermute | solution.py:205
  9.3 7.4 %collective-permute-start.1 = (f32[32,8,128]{2,1,0:T(8,128)S(1)}, f32[32,8,128]{2,1,0:T(8,128)S(1)}, u32[]{:S(2)}, u32[]{:S(2)}) collective-permute-start(f32[32,8,128]{2,1,0:T(8,128)S(1)} %get-tuple-element.40), channel_id=1, source_target_pairs={{0,8},{8,16},{16,24},{24,0},{32,40},{40,48},{48,56},{56,32},{64,72... | collective-permute-start | bytes 393224 | tf_op jit(solution)/shard_map/ppermute | solution.py:205
  9.3 7.4 %collective-permute-start.2 = (f32[32,8,128]{2,1,0:T(8,128)S(1)}, f32[32,8,128]{2,1,0:T(8,128)S(1)}, u32[]{:S(2)}, u32[]{:S(2)}) collective-permute-start(f32[32,8,128]{2,1,0:T(8,128)S(1)} %get-tuple-element.41), channel_id=1, source_target_pairs={{0,16},{8,24},{16,0},{24,8},{32,48},{40,56},{48,32},{56,40},{64,80... | collective-permute-start | bytes 393224 | tf_op jit(solution)/shard_map/ppermute | solution.py:205
  49.5 7.2 %collective-permute-start.3 = (f32[33,8,128]{2,1,0:T(8,128)S(1)}, f32[33,8,128]{2,1,0:T(8,128)S(1)}, u32[]{:S(2)}, u32[]{:S(2)}) collective-permute-start(f32[33,8,128]{2,1,0:T(8,128)S(1)} %get-tuple-element.45.send_ref), channel_id=1, source_target_pairs={{0,1},{1,0},{2,3},{3,2},{4,5},{5,4},{6,7},{7,6},{8,9},{9,8},{10,11... | collective-permute-start | bytes 405512 | tf_op jit(solution)/shard_map/ppermute | solution.py:275
  56.7 6.4 %collective-permute-start.6 = (f32[33,8,128]{2,1,0:T(8,128)S(1)}, f32[33,8,128]{2,1,0:T(8,128)S(1)}, u32[]{:S(2)}, u32[]{:S(2)}) collective-permute-start(f32[33,8,128]{2,1,0:T(8,128)S(1)} %add.3.refs_0_), channel_id=1, source_target_pairs={{0,4},{1,5},{2,6},{3,7},{4,0},{5,1},{6,2},{7,3},{8,12},{9,13},{10,... | collective-permute-start | bytes 405512 | tf_op jit(solution)/shard_map/ppermute | solution.py:282
  59.7 6.8 %collective-permute-start.5 = (f32[33,8,128]{2,1,0:T(8,128)S(1)}, f32[33,8,128]{2,1,0:T(8,128)S(1)}, u32[]{:S(2)}, u32[]{:S(2)}) collective-permute-start(f32[33,8,128]{2,1,0:T(8,128)S(1)} %add.3.refs_0_), channel_id=1, source_target_pairs={{0,2},{1,3},{2,4},{3,5},{4,6},{5,7},{6,0},{7,1},{8,10},{9,11},{10,... | collective-permute-start | bytes 405512 | tf_op jit(solution)/shard_map/ppermute | solution.py:282
  60.1 6.4 %collective-permute-start.4 = (f32[33,8,128]{2,1,0:T(8,128)S(1)}, f32[33,8,128]{2,1,0:T(8,128)S(1)}, u32[]{:S(2)}, u32[]{:S(2)}) collective-permute-start(f32[33,8,128]{2,1,0:T(8,128)S(1)} %add.3.refs_0_), channel_id=1, source_target_pairs={{0,6},{1,7},{2,0},{3,1},{4,2},{5,3},{6,4},{7,5},{8,14},{9,15},{10,... | collective-permute-start | bytes 405512 | tf_op jit(solution)/shard_map/ppermute | solution.py:282
  66.5 2.3 %collective-permute-start.7 = (f32[33,8,128]{2,1,0:T(8,128)S(1)}, f32[33,8,128]{2,1,0:T(8,128)S(1)}, u32[]{:S(2)}, u32[]{:S(2)}) collective-permute-start(f32[33,8,128]{2,1,0:T(8,128)S(1)} %sum_y.3.own0_ref), channel_id=1, source_target_pairs={{0,1},{1,0},{2,3},{3,2},{4,5},{5,4},{6,7},{7,6},{8,9},{9,8},{10,11... | collective-permute-start | bytes 405512 | tf_op jit(solution)/shard_map/ppermute | solution.py:284
  69.6 4.8 %collective-permute-start.8 = (f32[32,8,128]{2,1,0:T(8,128)S(1)}, f32[32,8,128]{2,1,0:T(8,128)S(1)}, u32[]{:S(2)}, u32[]{:S(2)}) collective-permute-start(f32[32,8,128]{2,1,0:T(8,128)S(1)} %get-tuple-element.47), channel_id=1, source_target_pairs={{0,24},{8,0},{16,8},{24,16},{32,56},{40,32},{48,40},{56,48},{64,88... | collective-permute-start | bytes 393224 | tf_op jit(solution)/shard_map/ppermute | solution.py:205
  71.2 6.8 %collective-permute-start.9 = (f32[32,8,128]{2,1,0:T(8,128)S(1)}, f32[32,8,128]{2,1,0:T(8,128)S(1)}, u32[]{:S(2)}, u32[]{:S(2)}) collective-permute-start(f32[32,8,128]{2,1,0:T(8,128)S(1)} %get-tuple-element.48), channel_id=1, source_target_pairs={{0,8},{8,16},{16,24},{24,0},{32,40},{40,48},{48,56},{56,32},{64,72... | collective-permute-start | bytes 393224 | tf_op jit(solution)/shard_map/ppermute | solution.py:205
  71.2 7.5 %collective-permute-start.10 = (f32[32,8,128]{2,1,0:T(8,128)S(1)}, f32[32,8,128]{2,1,0:T(8,128)S(1)}, u32[]{:S(2)}, u32[]{:S(2)}) collective-permute-start(f32[32,8,128]{2,1,0:T(8,128)S(1)} %get-tuple-element.49), channel_id=1, source_target_pairs={{0,16},{8,24},{16,0},{24,8},{32,48},{40,56},{48,32},{56,40},{64,80... | collective-permute-start | bytes 393224 | tf_op jit(solution)/shard_map/ppermute | solution.py:205
  106.9 6.6 %collective-permute-start.11 = (f32[33,8,128]{2,1,0:T(8,128)S(1)}, f32[33,8,128]{2,1,0:T(8,128)S(1)}, u32[]{:S(2)}, u32[]{:S(2)}) collective-permute-start(f32[33,8,128]{2,1,0:T(8,128)S(1)} %get-tuple-element.51.send_ref), channel_id=1, source_target_pairs={{0,1},{1,0},{2,3},{3,2},{4,5},{5,4},{6,7},{7,6},{8,9},{9,8},{10,11... | collective-permute-start | bytes 405512 | tf_op jit(solution)/shard_map/ppermute | solution.py:275
  113.6 6.4 %collective-permute-start.14 = (f32[33,8,128]{2,1,0:T(8,128)S(1)}, f32[33,8,128]{2,1,0:T(8,128)S(1)}, u32[]{:S(2)}, u32[]{:S(2)}) collective-permute-start(f32[33,8,128]{2,1,0:T(8,128)S(1)} %add.4.refs_0_), channel_id=1, source_target_pairs={{0,4},{1,5},{2,6},{3,7},{4,0},{5,1},{6,2},{7,3},{8,12},{9,13},{10,... | collective-permute-start | bytes 405512 | tf_op jit(solution)/shard_map/ppermute | solution.py:282
  115.4 8.0 %collective-permute-start.13 = (f32[33,8,128]{2,1,0:T(8,128)S(1)}, f32[33,8,128]{2,1,0:T(8,128)S(1)}, u32[]{:S(2)}, u32[]{:S(2)}) collective-permute-start(f32[33,8,128]{2,1,0:T(8,128)S(1)} %add.4.refs_0_), channel_id=1, source_target_pairs={{0,2},{1,3},{2,4},{3,5},{4,6},{5,7},{6,0},{7,1},{8,10},{9,11},{10,... | collective-permute-start | bytes 405512 | tf_op jit(solution)/shard_map/ppermute | solution.py:282
  116.8 6.6 %collective-permute-start.12 = (f32[33,8,128]{2,1,0:T(8,128)S(1)}, f32[33,8,128]{2,1,0:T(8,128)S(1)}, u32[]{:S(2)}, u32[]{:S(2)}) collective-permute-start(f32[33,8,128]{2,1,0:T(8,128)S(1)} %add.4.refs_0_), channel_id=1, source_target_pairs={{0,6},{1,7},{2,0},{3,1},{4,2},{5,3},{6,4},{7,5},{8,14},{9,15},{10,... | collective-permute-start | bytes 405512 | tf_op jit(solution)/shard_map/ppermute | solution.py:282
  123.5 2.0 %collective-permute-start.15 = (f32[33,8,128]{2,1,0:T(8,128)S(1)}, f32[33,8,128]{2,1,0:T(8,128)S(1)}, u32[]{:S(2)}, u32[]{:S(2)}) collective-permute-start(f32[33,8,128]{2,1,0:T(8,128)S(1)} %sum_y.4.own1_ref), channel_id=1, source_target_pairs={{0,1},{1,0},{2,3},{3,2},{4,5},{5,4},{6,7},{7,6},{8,9},{9,8},{10,11... | collective-permute-start | bytes 405512 | tf_op jit(solution)/shard_map/ppermute | solution.py:284
  126.4 5.0 %collective-permute-start.16 = (f32[33,8,128]{2,1,0:T(8,128)S(1)}, f32[33,8,128]{2,1,0:T(8,128)S(1)}, u32[]{:S(2)}, u32[]{:S(2)}) collective-permute-start(f32[33,8,128]{2,1,0:T(8,128)S(1)} %get-tuple-element.57), channel_id=1, source_target_pairs={{0,24},{8,0},{16,8},{24,16},{32,56},{40,32},{48,40},{56,48},{64,88... | collective-permute-start | bytes 405512 | tf_op jit(solution)/shard_map/ppermute | solution.py:205
  127.9 6.8 %collective-permute-start.17 = (f32[33,8,128]{2,1,0:T(8,128)S(1)}, f32[33,8,128]{2,1,0:T(8,128)S(1)}, u32[]{:S(2)}, u32[]{:S(2)}) collective-permute-start(f32[33,8,128]{2,1,0:T(8,128)S(1)} %get-tuple-element.58), channel_id=1, source_target_pairs={{0,8},{8,16},{16,24},{24,0},{32,40},{40,48},{48,56},{56,32},{64,72... | collective-permute-start | bytes 405512 | tf_op jit(solution)/shard_map/ppermute | solution.py:205
  128.0 7.7 %collective-permute-start.18 = (f32[33,8,128]{2,1,0:T(8,128)S(1)}, f32[33,8,128]{2,1,0:T(8,128)S(1)}, u32[]{:S(2)}, u32[]{:S(2)}) collective-permute-start(f32[33,8,128]{2,1,0:T(8,128)S(1)} %get-tuple-element.59), channel_id=1, source_target_pairs={{0,16},{8,24},{16,0},{24,8},{32,48},{40,56},{48,32},{56,40},{64,80... | collective-permute-start | bytes 405512 | tf_op jit(solution)/shard_map/ppermute | solution.py:205
  164.6 6.7 %collective-permute-start.19 = (f32[33,8,128]{2,1,0:T(8,128)S(1)}, f32[33,8,128]{2,1,0:T(8,128)S(1)}, u32[]{:S(2)}, u32[]{:S(2)}) collective-permute-start(f32[33,8,128]{2,1,0:T(8,128)S(1)} %get-tuple-element.64), channel_id=1, source_target_pairs={{0,1},{1,0},{2,3},{3,2},{4,5},{5,4},{6,7},{7,6},{8,9},{9,8},{10,11... | collective-permute-start | bytes 405512 | tf_op jit(solution)/shard_map/ppermute | solution.py:472
  170.2 25.5 %copy-start.1 = (f32[64]{0:T(128)S(1)}, f32[64]{0:T(128)}, u32[]{:S(2)}) copy-start(f32[64]{0:T(128)} %param.5) | copy-start | bytes 772
  171.3 24.4 %copy-start = (f32[1024,64]{0,1:T(8,128)S(1)}, f32[1024,64]{0,1:T(8,128)}, u32[]{:S(2)}) copy-start(f32[1024,64]{0,1:T(8,128)} %param.4) | copy-start | bytes 786436
  171.3 6.5 %collective-permute-start.22 = (f32[33,8,128]{2,1,0:T(8,128)S(1)}, f32[33,8,128]{2,1,0:T(8,128)S(1)}, u32[]{:S(2)}, u32[]{:S(2)}) collective-permute-start(f32[33,8,128]{2,1,0:T(8,128)S(1)} %add.5.refs_0_), channel_id=1, source_target_pairs={{0,4},{1,5},{2,6},{3,7},{4,0},{5,1},{6,2},{7,3},{8,12},{9,13},{10,... | collective-permute-start | bytes 405512 | tf_op jit(solution)/shard_map/ppermute | solution.py:282
  173.0 8.3 %collective-permute-start.21 = (f32[33,8,128]{2,1,0:T(8,128)S(1)}, f32[33,8,128]{2,1,0:T(8,128)S(1)}, u32[]{:S(2)}, u32[]{:S(2)}) collective-permute-start(f32[33,8,128]{2,1,0:T(8,128)S(1)} %add.5.refs_0_), channel_id=1, source_target_pairs={{0,2},{1,3},{2,4},{3,5},{4,6},{5,7},{6,0},{7,1},{8,10},{9,11},{10,... | collective-permute-start | bytes 405512 | tf_op jit(solution)/shard_map/ppermute | solution.py:282
  174.4 6.9 %collective-permute-start.20 = (f32[33,8,128]{2,1,0:T(8,128)S(1)}, f32[33,8,128]{2,1,0:T(8,128)S(1)}, u32[]{:S(2)}, u32[]{:S(2)}) collective-permute-start(f32[33,8,128]{2,1,0:T(8,128)S(1)} %add.5.refs_0_), channel_id=1, source_target_pairs={{0,6},{1,7},{2,0},{3,1},{4,2},{5,3},{6,4},{7,5},{8,14},{9,15},{10,... | collective-permute-start | bytes 405512 | tf_op jit(solution)/shard_map/ppermute | solution.py:282
  181.4 1.6 collective-permute-start.23
